TPU v7x, 256 devices: a whole 4x4x8 slice. The times are simulated.
256 devices in a mesh: lon: 16 (over z, y_lo), lat: 16 (over x, y_hi, core).
Axes of the slice: x: 4, y: 4 (y_hi: 2, y_lo: 2; y = y_hi * 2 + y_lo), z: 8, core: 2. Of those that a mesh axis runs over, the one named last changes fastest.
Arguments:
- latent: bfloat16 [256, 1024, 256], P('lat', 'lon'), may hold values from -6 to 6
- w_first: bfloat16 [3, 3, 256, 256], replicated, may hold values from -0.125 to 0.125
- w_second: bfloat16 [3, 3, 256, 256], replicated, may hold values from -0.125 to 0.125
- levels: int32 [256], replicated, may hold values from 3 to 9, as said below
- prior_scale: float32 [256], replicated, may hold values from 0.5 to 3
- bins: int32 [256, 1024, 256], P('lat', 'lon'), may hold values from 0 to 8, as said below
- code_grad: bfloat16 [256, 1024, 256], P('lat', 'lon'), may hold values from -6 to 6
Outputs:
- grad_latent: float32 [256, 1024, 256], P('lat', 'lon')
- grad_first: float32 [2304, 256], P('lon', 'lat')
- grad_second: float32 [2304, 256], P('lon', 'lat')
Inputs may be any that keep to these rules, and one draw needn't show every extreme that they name: `levels`: every level count is odd; each of 3, 5, 7 and 9 is held by a quarter of the channels. `bins`: each entry lies between 0 and its channel's level count minus 1.
All inputs are finite; a program needn't handle non-finite values.
Results may differ from a plain program's by a relative error of at most 0.0046.
Values may be sent and summed in bfloat16 or wider, within the bound.
No kernel may reach another device: no remote copies, remote signals or barrier semaphores. Data moves between devices by JAX's collectives and lax.ppermute only.
A program may use at most 64 MiB of HBM per device.

v0:
```python
import math

import jax
import jax.numpy as jnp
from jax import lax
from jax.sharding import PartitionSpec as P

RATE_WEIGHT = 0.5


def extended_2(cells, sides, width, closed):
    for axis, dim in sides:
        count = lax.axis_size(axis)
        ends = count if closed else count - 1
        head = lax.slice_in_dim(cells, 0, width, axis=dim)
        tail = lax.slice_in_dim(cells, cells.shape[dim] - width, cells.shape[dim], axis=dim)
        cells = jnp.concatenate(
            [
                lax.ppermute(tail, axis, [(i, (i + 1) % count) for i in range(ends)]),
                cells,
                lax.ppermute(head, axis, [((i + 1) % count, i) for i in range(ends)]),
            ],
            axis=dim,
        )
    return cells


def from_behind(value, axis, steps):
    count = lax.axis_size(axis)
    pairs = [(source, (source + steps) % count) for source in range(count)]
    return lax.ppermute(value, axis, pairs)


def passed_along(block, axis, distance):
    devices = range(lax.axis_size(axis))
    route = [(i - distance, i) for i in devices if i - distance in devices]
    return lax.ppermute(block, axis, route)


def extend(field):
    widened = extended_2(field, (("lon", 1),), 1, True)
    return extended_2(widened, (("lat", 0),), 1, False)


def across_pole(extended):
    half_loop = lax.axis_size("lon") // 2
    return from_behind((extended[1], extended[-2]), "lon", half_loop)


def sphere_pad(field):
    extended = extend(field)
    north_row, south_row = across_pole(extended)
    lat_index = lax.axis_index("lat")
    lat_count = lax.axis_size("lat")
    top_row = jnp.where(lat_index == 0, north_row, extended[0])
    bottom_row = jnp.where(lat_index == lat_count - 1, south_row, extended[-1])
    return jnp.concatenate([top_row[None], extended[1:-1], bottom_row[None]], axis=0)


def unfold(padded):
    lat_cells = padded.shape[0] - 2
    lon_cells = padded.shape[1] - 2
    return jnp.concatenate(
        [
            padded[row_off : row_off + lat_cells, col_off : col_off + lon_cells]
            for row_off in range(3)
            for col_off in range(3)
        ],
        axis=2,
    )


def flat_weight(weight):
    return weight.reshape(-1, weight.shape[3])


def weight_grad(patches, grad):
    return lax.dot_general(
        patches, grad, (((0, 1), (0, 1)), ((), ())), preferred_element_type=jnp.float32
    )


def transpose_return(grad, weight):
    channels = weight.shape[3]
    lat_cells = grad.shape[0]
    lon_cells = grad.shape[1]
    tap_terms = lax.dot_general(
        grad, flat_weight(weight), (((2,), (1,)), ((), ())), preferred_element_type=jnp.float32
    )
    padded = jnp.zeros((lat_cells + 2, lon_cells + 2, channels), jnp.float32)
    for row_off in range(3):
        for col_off in range(3):
            slot = 3 * row_off + col_off
            piece = tap_terms[:, :, slot * channels : (slot + 1) * channels]
            padded = padded + jnp.pad(
                piece, ((row_off, 2 - row_off), (col_off, 2 - col_off), (0, 0))
            )
    half_loop = lax.axis_size("lon") // 2
    lat_index = lax.axis_index("lat")
    lat_count = lax.axis_size("lat")
    north_back, south_back = from_behind((padded[0], padded[-1]), "lon", half_loop)
    from_above = passed_along(padded[-1], "lat", 1)
    from_below = passed_along(padded[0], "lat", -1)
    top_add = from_above + jnp.where(lat_index == 0, north_back, 0.0)
    bottom_add = from_below + jnp.where(lat_index == lat_count - 1, south_back, 0.0)
    interior = padded[1:-1]
    interior = interior.at[0].add(top_add)
    interior = interior.at[-1].add(bottom_add)
    from_west = from_behind(interior[:, -1], "lon", 1)
    from_east = from_behind(interior[:, 0], "lon", -1)
    central = interior[:, 1:-1]
    central = central.at[:, 0].add(from_west)
    central = central.at[:, -1].add(from_east)
    return central


def reduce_grads(grads):
    partial_rows = lax.psum_scatter(grads, "lon", scatter_dimension=0, tiled=True)
    return lax.psum_scatter(partial_rows, "lat", scatter_dimension=1, tiled=True)


def on_device(latent, w_first, w_second, levels, prior_scale, bins, code_grad):
    patches_latent = unfold(sphere_pad(latent))
    pre_act = jnp.dot(patches_latent, flat_weight(w_first), preferred_element_type=jnp.float32)
    activated = jax.nn.silu(pre_act).astype(jnp.bfloat16)
    patches_act = unfold(sphere_pad(activated))
    output = latent.astype(jnp.float32) + jnp.dot(
        patches_act, flat_weight(w_second), preferred_element_type=jnp.float32
    )
    bounded = jnp.tanh(output)
    half_levels = (levels.astype(jnp.float32) - 1.0) / 2.0
    centred = bins.astype(jnp.float32) - half_levels
    rate_slope = jnp.tanh(centred / (2.0 * prior_scale)) / prior_scale
    grad_out = (
        (code_grad.astype(jnp.float32) + RATE_WEIGHT * half_levels * rate_slope)
        * (1.0 - bounded * bounded)
    ).astype(jnp.bfloat16)
    grad_act = transpose_return(grad_out, w_second)
    sigmoid_pre = jax.nn.sigmoid(pre_act)
    grad_pre = (grad_act * sigmoid_pre * (1.0 + pre_act * (1.0 - sigmoid_pre))).astype(jnp.bfloat16)
    grad_latent = grad_out.astype(jnp.float32) + transpose_return(grad_pre, w_first)
    total_cells = latent.shape[0] * lax.axis_size("lat") * latent.shape[1] * lax.axis_size("lon")
    cell_scale = 1.0 / math.sqrt(total_cells)
    first_local = weight_grad(patches_latent, grad_pre) * cell_scale
    second_local = weight_grad(patches_act, grad_out) * cell_scale
    grad_first, grad_second = reduce_grads((first_local, second_local))
    return (grad_latent, grad_first, grad_second)


def solution(mesh):
    placed = (
        P("lat", "lon", None),
        P(),
        P(),
        P(),
        P(),
        P("lat", "lon", None),
        P("lat", "lon", None),
    )
    return jax.shard_map(
        on_device,
        mesh=mesh,
        in_specs=placed,
        out_specs=(P("lat", "lon", None), P("lon", "lat"), P("lon", "lat")),
        check_vma=False,
    )
```

profile of v0, /device:TPU:6, one launch (start us, length us, event | category | flops | bytes accessed | tf_op | source)
XLA Modules:
  0.0 393.5 jit_solution(4361573745377075881)
XLA Ops:
  9.9 5.4 %collective-permute-start.1 = (bf16[16,1,256]{2,1,0:T(2,128)(2,1)S(1)}, bf16[16,1,256]{2,1,0:T(2,128)(2,1)S(1)}, u32[]{:S(2)}, u32[]{:S(2)}) collective-permute-start(bf16[16,1,256]{2,1,0:T(2,128)(2,1)S(1)} %get-tuple-element.158), channel_id=1, source_target_pairs={{16,0},{32,16},{48,32},{64,48},{80,64},{96,80},{112,96},{128,112},... | collective-permute-start | bytes 24584 | tf_op jit(solution)/shard_map/ppermute | solution.py:21
  17.7 4.5 %collective-permute-start.2 = (bf16[66,256]{1,0:T(8,128)(2,1)S(1)}, bf16[66,256]{1,0:T(8,128)(2,1)S(1)}, u32[]{:S(2)}, u32[]{:S(2)}) collective-permute-start(bf16[66,256]{1,0:T(8,128)(2,1)S(1)} %bitcast.97), channel_id=1, source_target_pairs={{0,128},{16,144},{32,160},{48,176},{64,192},{80,208},{96,224},{112... | collective-permute-start | bytes 101384 | tf_op jit(solution)/shard_map/ppermute | solution.py:31
  24.2 6.0 %collective-permute-start.5 = (bf16[1,66,256]{2,1,0:T(8,128)(2,1)S(1)}, bf16[1,66,256]{2,1,0:T(8,128)(2,1)S(1)}, u32[]{:S(2)}, u32[]{:S(2)}) collective-permute-start(bf16[1,66,256]{2,1,0:T(8,128)(2,1)S(1)} %get-tuple-element.150), channel_id=1, source_target_pairs={{1,0},{2,1},{3,2},{4,3},{5,4},{6,5},{7,6},{8,7},{9,8},{10,9},{11,1... | collective-permute-start | bytes 101384 | tf_op jit(solution)/shard_map/ppermute | solution.py:21
  31.8 6.4 %collective-permute-done.4 = bf16[66,256]{1,0:T(8,128)(2,1)S(1)} collective-permute-done((bf16[66,256]{1,0:T(8,128)(2,1)S(1)}, bf16[66,256]{1,0:T(8,128)(2,1)S(1)}, u32[]{:S(2)}, u32[]{:S(2)}) %collective-permute-start.4) | collective-permute-done | bytes 33824 | tf_op jit(solution)/shard_map/ppermute | solution.py:31
  46.8 2.7 collective-permute-start.7
  54.6 6.0 %collective-permute-start.11 = (bf16[1,66,256]{2,0,1:T(2,128)(2,1)S(1)}, bf16[1,66,256]{2,0,1:T(2,128)(2,1)S(1)}, u32[]{:S(2)}, u32[]{:S(2)}) collective-permute-start(bf16[1,66,256]{2,0,1:T(2,128)(2,1)S(1)} %get-tuple-element.154), channel_id=1, source_target_pairs={{1,0},{2,1},{3,2},{4,3},{5,4},{6,5},{7,6},{8,7},{9,8},{10,9},{11,1... | collective-permute-start | bytes 101384 | tf_op jit(solution)/shard_map/ppermute | solution.py:21
  60.7 4.7 %collective-permute-start.10 = (bf16[66,256]{1,0:T(8,128)(2,1)S(1)}, bf16[66,256]{1,0:T(8,128)(2,1)S(1)}, u32[]{:S(2)}, u32[]{:S(2)}) collective-permute-start(bf16[66,256]{1,0:T(8,128)(2,1)S(1)} %bitcast.99), channel_id=1, source_target_pairs={{0,128},{16,144},{32,160},{48,176},{64,192},{80,208},{96,224},{112... | collective-permute-start | bytes 101384 | tf_op jit(solution)/shard_map/ppermute | solution.py:31
  65.5 3.3 collective-permute-done.10
  71.7 2.4 fusion.6
  74.1 3.0 fusion.1
  80.8 2.6 pad_add_fusion.1
  83.4 4.6 %collective-permute-start.13 = (f32[66,256]{1,0:T(8,128)S(1)}, f32[66,256]{1,0:T(8,128)S(1)}, u32[]{:S(2)}, u32[]{:S(2)}) collective-permute-start(f32[66,256]{1,0:T(8,128)S(1)} %get-tuple-element.140), channel_id=1, source_target_pairs={{0,128},{16,144},{32,160},{48,176},{64,192},{80,208},{96,224},{112... | collective-permute-start | bytes 202760 | tf_op jit(solution)/shard_map/ppermute | solution.py:31
  89.9 6.0 %collective-permute-start.14 = (f32[66,256]{1,0:T(8,128)S(1)}, f32[66,256]{1,0:T(8,128)S(1)}, u32[]{:S(2)}, u32[]{:S(2)}) collective-permute-start(f32[66,256]{1,0:T(8,128)S(1)} %get-tuple-element.140), channel_id=1, source_target_pairs={{1,0},{2,1},{3,2},{4,3},{5,4},{6,5},{7,6},{8,7},{9,8},{10,9},{11,1... | collective-permute-start | bytes 202760 | tf_op jit(solution)/shard_map/ppermute | solution.py:37
  98.0 6.3 %collective-permute-done.15 = f32[66,256]{1,0:T(8,128)S(1)} collective-permute-done((f32[66,256]{1,0:T(8,128)S(1)}, f32[66,256]{1,0:T(8,128)S(1)}, u32[]{:S(2)}, u32[]{:S(2)}) %collective-permute-start.15) | collective-permute-done | bytes 67616 | tf_op jit(solution)/shard_map/ppermute | solution.py:31
  104.4 2.8 scatter-add.29
  108.9 3.0 collective-permute-start.17
  116.1 5.2 %fusion = f32[2304,256]{1,0:T(8,128)} fusion(bf16[16,64,2304]{2,1,0:T(8,128)(2,1)} %copy-done.7, bf16[16,64,256]{2,0,1:T(8,128)(2,1)S(1)} %multiply_convert_fusion), kind=kOutput, calls=%fused_computation.1 | convolution fusion | flops 1208549376 | bytes 7602176 | tf_op jit(solution)/shard_map/dot_general | solution.py:78
  129.0 6.0 %collective-permute-start.20 = (f32[66,256]{1,0:T(8,128)S(1)}, f32[66,256]{1,0:T(8,128)S(1)}, u32[]{:S(2)}, u32[]{:S(2)}) collective-permute-start(f32[66,256]{1,0:T(8,128)S(1)} %get-tuple-element.138), channel_id=1, source_target_pairs={{1,0},{2,1},{3,2},{4,3},{5,4},{6,5},{7,6},{8,7},{9,8},{10,9},{11,1... | collective-permute-start | bytes 202760 | tf_op jit(solution)/shard_map/ppermute | solution.py:37
  135.1 6.0 %collective-permute-start.21 = (f32[66,256]{1,0:T(8,128)S(1)}, f32[66,256]{1,0:T(8,128)S(1)}, u32[]{:S(2)}, u32[]{:S(2)}) collective-permute-start(f32[66,256]{1,0:T(8,128)S(1)} %get-tuple-element.139), channel_id=1, source_target_pairs={{0,128},{16,144},{32,160},{48,176},{64,192},{80,208},{96,224},{112... | collective-permute-start | bytes 202760 | tf_op jit(solution)/shard_map/ppermute | solution.py:31
  146.1 3.3 collective-permute-start.23
  150.5 4.7 %reduce-scatter.11.cloned.1.call-done = f32[144,256]{1,0:T(8,128)} async-done(((f32[2304,256]{1,0:T(8,128)}), f32[144,256]{1,0:T(8,128)}) %reduce-scatter.11.cloned.1.call-update) | async-done | bytes 147472 | tf_op jit(solution)/shard_map/reduce_scatter | solution.py:118
  157.0 76.6 %reduce-scatter.9.cloned.1.call-done = f32[144,256]{1,0:T(8,128)} async-done(((f32[2304,256]{1,0:T(8,128)}), f32[144,256]{1,0:T(8,128)}) %reduce-scatter.9.cloned.1.call-update) | async-done | bytes 147472 | tf_op jit(solution)/shard_map/reduce_scatter | solution.py:118
  237.2 73.0 %reduce-scatter.15.cloned.1.call-done = f32[16,144]{1,0:T(8,128)} async-done(((f32[256,144]{1,0:T(8,128)}), f32[16,144]{1,0:T(8,128)}) %reduce-scatter.15.cloned.1.call-update) | async-done | bytes 9232
  310.2 76.8 %reduce-scatter.13.cloned.1.call-done = f32[16,144]{1,0:T(8,128)} async-done(((f32[256,144]{1,0:T(8,128)}), f32[16,144]{1,0:T(8,128)}) %reduce-scatter.13.cloned.1.call-update) | async-done | bytes 9232
  (133 shorter events, 57.7 us)
Async XLA Ops:
  7.2 148.0 %reduce-scatter.11.cloned.1.call-start = ((), (), s32[]{:S(2)}) async-start(), calls=%async_computation.5 | async-start | bytes 2506752 | tf_op jit(solution)/shard_map/reduce_scatter | solution.py:118
  8.2 8.7 %collective-permute-start = (bf16[16,1,256]{2,1,0:T(2,128)(2,1)S(1)}, bf16[16,1,256]{2,1,0:T(2,128)(2,1)S(1)}, u32[]{:S(2)}, u32[]{:S(2)}) collective-permute-start(bf16[16,1,256]{2,1,0:T(2,128)(2,1)S(1)} %get-tuple-element.157), channel_id=1, source_target_pairs={{0,16},{16,32},{32,48},{48,64},{64,80},{80,96},{96,112},{112,128},... | collective-permute-start | bytes 24584 | tf_op jit(solution)/shard_map/ppermute | solution.py:19
  9.9 7.0 %collective-permute-start.1 = (bf16[16,1,256]{2,1,0:T(2,128)(2,1)S(1)}, bf16[16,1,256]{2,1,0:T(2,128)(2,1)S(1)}, u32[]{:S(2)}, u32[]{:S(2)}) collective-permute-start(bf16[16,1,256]{2,1,0:T(2,128)(2,1)S(1)} %get-tuple-element.158), channel_id=1, source_target_pairs={{16,0},{32,16},{48,32},{64,48},{80,64},{96,80},{112,96},{128,112},... | collective-permute-start | bytes 24584 | tf_op jit(solution)/shard_map/ppermute | solution.py:21
  17.7 14.1 %collective-permute-start.2 = (bf16[66,256]{1,0:T(8,128)(2,1)S(1)}, bf16[66,256]{1,0:T(8,128)(2,1)S(1)}, u32[]{:S(2)}, u32[]{:S(2)}) collective-permute-start(bf16[66,256]{1,0:T(8,128)(2,1)S(1)} %bitcast.97), channel_id=1, source_target_pairs={{0,128},{16,144},{32,160},{48,176},{64,192},{80,208},{96,224},{112... | collective-permute-start | bytes 101384 | tf_op jit(solution)/shard_map/ppermute | solution.py:31
  22.2 9.6 %collective-permute-start.3 = (bf16[1,66,256]{2,1,0:T(8,128)(2,1)S(1)}, bf16[1,66,256]{2,1,0:T(8,128)(2,1)S(1)}, u32[]{:S(2)}, u32[]{:S(2)}) collective-permute-start(bf16[1,66,256]{2,1,0:T(8,128)(2,1)S(1)} %get-tuple-element.149), channel_id=1, source_target_pairs={{0,1},{1,2},{2,3},{3,4},{4,5},{5,6},{6,7},{7,8},{8,9},{9,10},{10,1... | collective-permute-start | bytes 101384 | tf_op jit(solution)/shard_map/ppermute | solution.py:19
  24.2 14.0 %collective-permute-start.5 = (bf16[1,66,256]{2,1,0:T(8,128)(2,1)S(1)}, bf16[1,66,256]{2,1,0:T(8,128)(2,1)S(1)}, u32[]{:S(2)}, u32[]{:S(2)}) collective-permute-start(bf16[1,66,256]{2,1,0:T(8,128)(2,1)S(1)} %get-tuple-element.150), channel_id=1, source_target_pairs={{1,0},{2,1},{3,2},{4,3},{5,4},{6,5},{7,6},{8,7},{9,8},{10,9},{11,1... | collective-permute-start | bytes 101384 | tf_op jit(solution)/shard_map/ppermute | solution.py:21
  30.2 8.0 %collective-permute-start.4 = (bf16[66,256]{1,0:T(8,128)(2,1)S(1)}, bf16[66,256]{1,0:T(8,128)(2,1)S(1)}, u32[]{:S(2)}, u32[]{:S(2)}) collective-permute-start(bf16[66,256]{1,0:T(8,128)(2,1)S(1)} %bitcast.98), channel_id=1, source_target_pairs={{0,128},{16,144},{32,160},{48,176},{64,192},{80,208},{96,224},{112... | collective-permute-start | bytes 101384 | tf_op jit(solution)/shard_map/ppermute | solution.py:31
  51.1 14.3 %collective-permute-start.8 = (bf16[66,256]{1,0:T(8,128)(2,1)S(1)}, bf16[66,256]{1,0:T(8,128)(2,1)S(1)}, u32[]{:S(2)}, u32[]{:S(2)}) collective-permute-start(bf16[66,256]{1,0:T(8,128)(2,1)S(1)} %bitcast.100), channel_id=1, source_target_pairs={{0,128},{16,144},{32,160},{48,176},{64,192},{80,208},{96,224},{112... | collective-permute-start | bytes 101384 | tf_op jit(solution)/shard_map/ppermute | solution.py:31
  52.7 12.7 %collective-permute-start.9 = (bf16[1,66,256]{2,0,1:T(2,128)(2,1)S(1)}, bf16[1,66,256]{2,0,1:T(2,128)(2,1)S(1)}, u32[]{:S(2)}, u32[]{:S(2)}) collective-permute-start(bf16[1,66,256]{2,0,1:T(2,128)(2,1)S(1)} %get-tuple-element.153), channel_id=1, source_target_pairs={{0,1},{1,2},{2,3},{3,4},{4,5},{5,6},{6,7},{7,8},{8,9},{9,10},{10,1... | collective-permute-start | bytes 101384 | tf_op jit(solution)/shard_map/ppermute | solution.py:19
  54.6 14.2 %collective-permute-start.11 = (bf16[1,66,256]{2,0,1:T(2,128)(2,1)S(1)}, bf16[1,66,256]{2,0,1:T(2,128)(2,1)S(1)}, u32[]{:S(2)}, u32[]{:S(2)}) collective-permute-start(bf16[1,66,256]{2,0,1:T(2,128)(2,1)S(1)} %get-tuple-element.154), channel_id=1, source_target_pairs={{1,0},{2,1},{3,2},{4,3},{5,4},{6,5},{7,6},{8,7},{9,8},{10,9},{11,1... | collective-permute-start | bytes 101384 | tf_op jit(solution)/shard_map/ppermute | solution.py:21
  60.7 8.1 %collective-permute-start.10 = (bf16[66,256]{1,0:T(8,128)(2,1)S(1)}, bf16[66,256]{1,0:T(8,128)(2,1)S(1)}, u32[]{:S(2)}, u32[]{:S(2)}) collective-permute-start(bf16[66,256]{1,0:T(8,128)(2,1)S(1)} %bitcast.99), channel_id=1, source_target_pairs={{0,128},{16,144},{32,160},{48,176},{64,192},{80,208},{96,224},{112... | collective-permute-start | bytes 101384 | tf_op jit(solution)/shard_map/ppermute | solution.py:31
  77.1 156.6 %reduce-scatter.9.cloned.1.call-start = ((), (), s32[]{:S(2)}) async-start(), calls=%async_computation.4 | async-start | bytes 2506752 | tf_op jit(solution)/shard_map/reduce_scatter | solution.py:118
  83.4 14.2 %collective-permute-start.13 = (f32[66,256]{1,0:T(8,128)S(1)}, f32[66,256]{1,0:T(8,128)S(1)}, u32[]{:S(2)}, u32[]{:S(2)}) collective-permute-start(f32[66,256]{1,0:T(8,128)S(1)} %get-tuple-element.140), channel_id=1, source_target_pairs={{0,128},{16,144},{32,160},{48,176},{64,192},{80,208},{96,224},{112... | collective-permute-start | bytes 202760 | tf_op jit(solution)/shard_map/ppermute | solution.py:31
  88.0 9.6 %collective-permute-start.12 = (f32[66,256]{1,0:T(8,128)S(1)}, f32[66,256]{1,0:T(8,128)S(1)}, u32[]{:S(2)}, u32[]{:S(2)}) collective-permute-start(f32[66,256]{1,0:T(8,128)S(1)} %get-tuple-element.141), channel_id=1, source_target_pairs={{0,1},{1,2},{2,3},{3,4},{4,5},{5,6},{6,7},{7,8},{8,9},{9,10},{10,1... | collective-permute-start | bytes 202760 | tf_op jit(solution)/shard_map/ppermute | solution.py:37
  89.9 8.1 %collective-permute-start.14 = (f32[66,256]{1,0:T(8,128)S(1)}, f32[66,256]{1,0:T(8,128)S(1)}, u32[]{:S(2)}, u32[]{:S(2)}) collective-permute-start(f32[66,256]{1,0:T(8,128)S(1)} %get-tuple-element.140), channel_id=1, source_target_pairs={{1,0},{2,1},{3,2},{4,3},{5,4},{6,5},{7,6},{8,7},{9,8},{10,9},{11,1... | collective-permute-start | bytes 202760 | tf_op jit(solution)/shard_map/ppermute | solution.py:37
  95.9 8.3 %collective-permute-start.15 = (f32[66,256]{1,0:T(8,128)S(1)}, f32[66,256]{1,0:T(8,128)S(1)}, u32[]{:S(2)}, u32[]{:S(2)}) collective-permute-start(f32[66,256]{1,0:T(8,128)S(1)} %get-tuple-element.141), channel_id=1, source_target_pairs={{0,128},{16,144},{32,160},{48,176},{64,192},{80,208},{96,224},{112... | collective-permute-start | bytes 202760 | tf_op jit(solution)/shard_map/ppermute | solution.py:31
  121.4 188.9 %reduce-scatter.15.cloned.1.call-start = ((), (), s32[]{:S(2)}) async-start(), calls=%async_computation.7 | async-start | bytes 278528
  127.0 14.2 %collective-permute-start.19 = (f32[66,256]{1,0:T(8,128)S(1)}, f32[66,256]{1,0:T(8,128)S(1)}, u32[]{:S(2)}, u32[]{:S(2)}) collective-permute-start(f32[66,256]{1,0:T(8,128)S(1)} %get-tuple-element.138), channel_id=1, source_target_pairs={{0,128},{16,144},{32,160},{48,176},{64,192},{80,208},{96,224},{112... | collective-permute-start | bytes 202760 | tf_op jit(solution)/shard_map/ppermute | solution.py:31
  127.1 14.1 %collective-permute-start.18 = (f32[66,256]{1,0:T(8,128)S(1)}, f32[66,256]{1,0:T(8,128)S(1)}, u32[]{:S(2)}, u32[]{:S(2)}) collective-permute-start(f32[66,256]{1,0:T(8,128)S(1)} %get-tuple-element.139), channel_id=1, source_target_pairs={{0,1},{1,2},{2,3},{3,4},{4,5},{5,6},{6,7},{7,8},{8,9},{9,10},{10,1... | collective-permute-start | bytes 202760 | tf_op jit(solution)/shard_map/ppermute | solution.py:37
  129.0 12.2 %collective-permute-start.20 = (f32[66,256]{1,0:T(8,128)S(1)}, f32[66,256]{1,0:T(8,128)S(1)}, u32[]{:S(2)}, u32[]{:S(2)}) collective-permute-start(f32[66,256]{1,0:T(8,128)S(1)} %get-tuple-element.138), channel_id=1, source_target_pairs={{1,0},{2,1},{3,2},{4,3},{5,4},{6,5},{7,6},{8,7},{9,8},{10,9},{11,1... | collective-permute-start | bytes 202760 | tf_op jit(solution)/shard_map/ppermute | solution.py:37
  135.1 8.3 %collective-permute-start.21 = (f32[66,256]{1,0:T(8,128)S(1)}, f32[66,256]{1,0:T(8,128)S(1)}, u32[]{:S(2)}, u32[]{:S(2)}) collective-permute-start(f32[66,256]{1,0:T(8,128)S(1)} %get-tuple-element.139), channel_id=1, source_target_pairs={{0,128},{16,144},{32,160},{48,176},{64,192},{80,208},{96,224},{112... | collective-permute-start | bytes 202760 | tf_op jit(solution)/shard_map/ppermute | solution.py:31
  143.5 7.0 %collective-permute-start.22 = (f32[16,256]{1,0:T(8,128)S(1)}, f32[16,256]{1,0:T(8,128)S(1)}, u32[]{:S(2)}, u32[]{:S(2)}) collective-permute-start(f32[16,256]{1,0:T(8,128)S(1)} %bitcast.102), channel_id=1, source_target_pairs={{0,16},{16,32},{32,48},{48,64},{64,80},{80,96},{96,112},{112,128},... | collective-permute-start | bytes 49160 | tf_op jit(solution)/shard_map/ppermute | solution.py:31
  146.1 10.9 %collective-permute-start.23 = (f32[16,256]{1,0:T(8,128)S(1)}, f32[16,256]{1,0:T(8,128)S(1)}, u32[]{:S(2)}, u32[]{:S(2)}) collective-permute-start(f32[16,256]{1,0:T(8,128)S(1)} %bitcast.101), channel_id=1, source_target_pairs={{0,240},{16,0},{32,16},{48,32},{64,48},{80,64},{96,80},{112,96},{1... | collective-permute-start | bytes 49160 | tf_op jit(solution)/shard_map/ppermute | solution.py:31
  157.0 230.0 %reduce-scatter.13.cloned.1.call-start = ((), (), s32[]{:S(2)}) async-start(), calls=%async_computation.6 | async-start | bytes 278528
  (16 other events, 356.4 us)
Sparse Core Ops, SparseCore 0:
  77.2 77.9 reduce-scatter.10
  157.7 75.8 reduce-scatter.8
  238.2 71.9 reduce-scatter.14
  315.2 71.7 reduce-scatter.12
where the time goes:
time: 394 us
  waiting for transfers between devices  257 us (65%)
  starting transfers between devices  77.8 us (20%)
  local copies, waits for them, and re-layouts  19 us (5%)
  matrix products  14.9 us (4%)
  between operations  14.4 us (4%)
  other arithmetic  10.5 us (3%)
    unnamed x6, waiting for transfers between devices  150 us
    reduce_scatter x2, waiting for transfers between devices, reduce_grads(): lax.psum_scatter(grads, 'lon', scatter_dimension=0, tiled=True)  81.3 us
    ppermute x12, starting transfers between devices, from_behind(): return lax.ppermute(value, axis, pairs)  34.4 us
    ppermute x12, waiting for transfers between devices, from_behind(): return lax.ppermute(value, axis, pairs)  22.5 us
    ppermute x4, starting transfers between devices, extended_2(): lax.ppermute(head, axis, [((i + 1) % count, i) for i in range(ends)])  20.1 us
    ppermute x4, starting transfers between devices, passed_along(): return lax.ppermute(block, axis, route)  15.9 us
    unnamed x43, local copies, waits for them, and re-layouts  10.3 us
    dot_general x2, matrix products, weight_grad(): lax.dot_general(patches, grad, (((0, 1), (0, 1)), ((), ())), preferred_el...  8.21 us
  transfers between devices with their start and end apart: 28, of which 13 were waited for; matrix products, arithmetic and copies ran while one was open for 7% of the time, Pallas kernels for 0%

commit v1 on v0

v1 whole, which is shorter than its diff:
```python
import math

import jax
import jax.numpy as jnp
from jax import lax
from jax.experimental import pallas as pl
from jax.experimental.pallas import tpu as pltpu
from jax.sharding import PartitionSpec as P

RATE_WEIGHT = 0.5

F32 = jnp.float32
BF16 = jnp.bfloat16

C = 256
ROWS = 16
COLS = 64
RIM = 4
EXT = ROWS + 2 * RIM
W = 80
N = EXT * W + 16
BASE = 8
TAPS = 2304


def lon_lat():
    return lax.axis_index("lon"), lax.axis_index("lat")


def ring_pairs(step):
    pairs = []
    for lon in range(8):
        circle = [(lon, lat) for lat in range(16)] + [(lon + 8, lat) for lat in reversed(range(16))]
        for i, (lo, la) in enumerate(circle):
            tlo, tla = circle[(i + step) % 32]
            pairs.append((lo * 16 + la, tlo * 16 + tla))
    return pairs


def moved(block, route):
    pairs = []
    for lon in range(16):
        for lat in range(16):
            z, yl, x, yh, core = route(lon // 2, lon % 2, lat // 4, lat // 2 % 2, lat % 2)
            pairs.append((lon * 16 + lat, (z * 2 + yl) * 16 + x * 4 + yh * 2 + core))
    return lax.ppermute(block, ("lon", "lat"), pairs)


def facing(first, second, lon_low, rows, count, mirrored):
    picked = []
    for k in range(count):
        at = rows + jnp.where(mirrored, count - 1 - k, k)
        picked.append(jnp.where(lon_low, first[at].astype(F32), second[at].astype(F32)))
    return picked


def strips_kernel(latent, code, bins, cw, ccw, east, west):
    lon, lat = lon_lat()
    low = lon < 8
    spot = lax.broadcasted_iota(jnp.int32, (EXT * 8, C), 0) % 8

    def gathered(own, start, count, right):
        north = facing(cw, ccw, low, start, count, lat == 0)
        south = facing(ccw, cw, low, start, count, lat == 15)
        cut = slice(56, 64) if right else slice(0, 8)
        wide = own[:, 48:64, :].astype(F32)[:, 8:16] if right else own[:, 0:16, :].astype(F32)[:, 0:8]
        fill = [jnp.zeros((8, C), F32)] * (RIM - count)
        rows = fill + [v[cut] for v in north] + [wide[r] for r in range(ROWS)] + [v[cut] for v in south] + fill
        return jnp.concatenate(rows, axis=0)

    def turned(value, by):
        return pltpu.roll(value, by % (EXT * 8), 0)

    for out, right in ((east, True), (west, False)):
        a = gathered(latent, 0, 4, right)
        b = gathered(code, 4, 2, right)
        c = gathered(bins, 6, 2, right)
        if right:
            a, b = turned(a, -4), turned(b, -2)
        else:
            b, c = turned(b, 4), turned(c, 6)
        out[...] = jnp.where(spot < 4, a, jnp.where(spot < 6, b, c)).astype(BF16)


def put(ref, at, value):
    rows = value.shape[0]
    ref[0, BASE + at : BASE + at + rows, :] = value[:, :128]
    ref[1, BASE + at : BASE + at + rows, :] = value[:, 128:]


def get(ref, at, rows):
    return jnp.concatenate([ref[0, BASE + at : BASE + at + rows, :], ref[1, BASE + at : BASE + at + rows, :]], axis=1)


def spread(dest, ref, start, stop):
    for at in range(start, stop, 320):
        rows = min(320, stop - at)
        for b in range(3):
            for half in range(2):
                lane = b * 256 + half * 128
                dest[at : at + rows, lane : lane + 128] = ref[half, pl.ds(BASE + at + b - 1, rows), :].astype(BF16)


def block_kernel(
    latent, code, bins, cw, ccw, from_east, from_west, w1, w2, w1t, w2t, levels, prior,
    grad_latent, send, keep,
    x32, q32, a32, g32, p32, dact, lat3, act3, go3, gp3, turn,
):
    lon, lat = lon_lat()
    low = lon < 8
    at_north = lat == 0
    at_south = lat == 15
    core = lat % 2

    half_levels = (levels[...].astype(F32) - 1.0) / 2.0
    scale = prior[...]
    double = 2.0 * scale
    weight = RATE_WEIGHT * half_levels

    def cotangent(code_part, bins_part):
        slope = jnp.tanh((bins_part - half_levels) / double) / scale
        return code_part + weight * slope

    north = facing(cw, ccw, low, 0, 4, at_north)
    south = facing(ccw, cw, low, 0, 4, at_south)
    for k in range(4):
        put(x32, k * W + 16, north[k])
        put(x32, (20 + k) * W + 16, south[k])
    for r in range(ROWS):
        put(x32, (4 + r) * W + 16, latent[r].astype(F32))
    north_code = facing(cw, ccw, low, 4, 2, at_north)
    south_code = facing(ccw, cw, low, 4, 2, at_south)
    north_bins = facing(cw, ccw, low, 6, 2, at_north)
    south_bins = facing(ccw, cw, low, 6, 2, at_south)
    for k in range(2):
        put(q32, (2 + k) * W + 16, cotangent(north_code[k], north_bins[k]))
        put(q32, (20 + k) * W + 16, cotangent(south_code[k], south_bins[k]))
    for r in range(ROWS):
        put(q32, (4 + r) * W + 16, cotangent(code[r].astype(F32), bins[r].astype(F32)))

    rows = EXT * 8
    spot = lax.broadcasted_iota(jnp.int32, (rows, C), 0) % 8
    right = from_east[...].astype(F32)
    left = from_west[...].astype(F32)

    def turned(value, by):
        return pltpu.roll(value, by % rows, 0)

    right_x = jnp.where(spot < 4, right, 0.0)
    left_x = jnp.where(spot >= 4, turned(left, 4), 0.0)
    right_q = jnp.where(spot < 2, cotangent(turned(right, -4), turned(right, -6)), 0.0)
    left_q = jnp.where(spot >= 6, cotangent(turned(left, 2), left), 0.0)
    blank = jnp.zeros((8, C), F32)
    put(x32, -8, blank)
    put(x32, 0, blank)
    put(x32, N - 8, blank)
    put(x32, N, blank)
    for r in range(EXT):
        part = slice(r * 8, r * 8 + 8)
        put(x32, (r + 1) * W, right_x[part])
        put(x32, r * W + 8, left_x[part])
        if 2 <= r < 22:
            put(q32, (r + 1) * W, right_q[part])
            put(q32, r * W + 8, left_q[part])
    put(q32, 2 * W, blank)
    put(q32, 22 * W + 8, blank)

    def product(source, at, count, weights, order):
        total = None
        for slot in range(3):
            begin = order[slot]
            if not isinstance(begin, int):
                begin = pl.multiple_of(begin, 256)
            piece = jnp.dot(
                source[at + (slot - 1) * W : at + (slot - 1) * W + count, :],
                weights[pl.ds(begin, 768), :],
                preferred_element_type=F32,
            )
            total = piece if total is None else total + piece
        return total

    plain = (0, 768, 1536)
    top_flip = (jnp.where(at_north, 1536, 0), 768, jnp.where(at_north, 0, 1536))
    low_flip = (jnp.where(at_south, 1536, 0), 768, jnp.where(at_south, 0, 1536))
    above_flip = (jnp.where(at_north, 1536, 0), 768, 1536)
    below_flip = (0, 768, jnp.where(at_south, 0, 1536))

    def pieces(first, last, top, bottom, orders):
        cuts = [(first, top, orders[0])]
        middle = (bottom - top) // 2
        cuts += [(top, top + middle, plain), (top + middle, bottom, plain)]
        cuts += [(bottom, last, orders[1])]
        out = []
        for i, (start, stop, order) in enumerate(cuts):
            out.append((start * W, (stop - start) * W + 16, 8 if i else 0, order))
        return out

    spread(lat3, x32, 0, N)
    for at, count, skip, order in pieces(1, 23, 4, 20, (top_flip, low_flip)):
        pre = product(lat3, at, count, w1, order)[skip:]
        sig = jax.nn.sigmoid(pre)
        put(dact, at + skip, sig * (1.0 + pre * (1.0 - sig)))
        put(a32, at + skip, pre * sig)

    spread(act3, a32, W, 23 * W + 16)
    for at, count, skip, order in pieces(2, 22, 4, 20, (top_flip, low_flip)):
        conv = product(act3, at, count, w2, order)[skip:]
        size = count - skip
        bounded = jnp.tanh(get(x32, at + skip, size) + conv)
        out = get(q32, at + skip, size) * (1.0 - bounded * bounded)
        put(g32, at + skip, out.astype(BF16).astype(F32))

    def own_cells(source, shift):
        return jnp.concatenate(
            [source[(r + shift) * W + 16 : (r + shift) * W + 80, :] for r in range(4, 20)], axis=0
        )

    def weight_grad(source, grad3, lane):
        turn[...] = jnp.transpose(own_cells(grad3.at[:, 256:512], 0))
        for a in range(3):
            full = jnp.dot(turn[...], own_cells(source, a - 1), preferred_element_type=F32)
            full = full.reshape(8, 2, 16, 768) * (1.0 / 512.0)
            mine = jnp.where(core == 0, full[:, 0], full[:, 1])
            other = jnp.where(core == 0, full[:, 1], full[:, 0])
            keep[:, :, lane + 768 * a : lane + 768 * (a + 1)] = mine
            send[:, :, lane + 768 * a : lane + 768 * (a + 1)] = other.astype(BF16)

    spread(go3, g32, 2 * W, 22 * W + 16)
    weight_grad(act3, go3, TAPS)

    for at, count, skip, order in pieces(3, 21, 5, 19, (above_flip, below_flip)):
        back = product(go3, at, count, w2t, order)[skip:]
        grad = back * get(dact, at + skip, count - skip)
        put(p32, at + skip, grad)

    spread(gp3, p32, 3 * W, 21 * W + 16)
    weight_grad(lat3, gp3, 0)

    def rows_of(first, count):
        return jnp.concatenate([gp3[r * W + 16 : r * W + 80, :] for r in range(first, first + count)], axis=0)

    def tapped(first, count, begin):
        if not isinstance(begin, int):
            begin = pl.multiple_of(begin, 256)
        return jnp.dot(rows_of(first, count), w1t[pl.ds(begin, 768), :], preferred_element_type=F32)

    above = jnp.concatenate([tapped(3, 1, above_flip[0]), tapped(4, 15, 0)], axis=0)
    below = jnp.concatenate([tapped(5, 15, 1536), tapped(20, 1, below_flip[2])], axis=0)
    total = tapped(4, 16, 768) + above + below
    for r in range(ROWS):
        grad_latent[r] = total[r * COLS : (r + 1) * COLS] + get(g32, (4 + r) * W + 16, COLS)


def after_core_kernel(keep, got, own, s1, s2, s3):
    lon, lat = lon_lat()
    x = lat // 4

    def part(to):
        return keep[pl.ds(2 * to, 2)] + got[pl.ds(2 * to, 2)].astype(F32)

    own[...] = part(x)
    for k, out in ((1, s1), (2, s2), (3, s3)):
        out[...] = part((x + k) % 4).astype(BF16)


def after_x_kernel(own_in, r1, r2, r3, own, s1, s2, s3, parts):
    lon, lat = lon_lat()
    yl, yh = lon % 2, lat // 2 % 2
    for h in range(2):
        total = own_in[h] + r1[h].astype(F32) + r2[h].astype(F32) + r3[h].astype(F32)
        for tensor in range(2):
            for j in range(16):
                lane = tensor * TAPS + 144 * j
                parts[j % 2, h, j // 2, 16 * tensor : 16 * tensor + 16, :] = total[:, lane : lane + 144]
    own[...] = parts[yl, yh]
    s1[...] = parts[1 - yl, yh].astype(BF16)
    s2[...] = parts[yl, 1 - yh].astype(BF16)
    s3[...] = parts[1 - yl, 1 - yh].astype(BF16)


def after_y_kernel(own_in, r1, r2, r3, own, s1):
    lon, lat = lon_lat()
    odd = lon // 2 % 2
    for k in range(4):
        even_part = own_in[2 * k] + r1[2 * k].astype(F32) + r2[2 * k].astype(F32) + r3[2 * k].astype(F32)
        odd_part = own_in[2 * k + 1] + r1[2 * k + 1].astype(F32) + r2[2 * k + 1].astype(F32) + r3[2 * k + 1].astype(F32)
        own[k] = jnp.where(odd == 0, even_part, odd_part)
        s1[k] = jnp.where(odd == 0, odd_part, even_part)


def after_pair_kernel(own_in, r1, own, s1, s2, s3):
    lon, lat = lon_lat()
    far = lon // 4
    own[...] = own_in[far] + r1[far]
    for k, out in ((1, s1), (2, s2), (3, s3)):
        to = (far + k) % 4
        out[...] = own_in[to] + r1[to]


def last_kernel(own_in, r1, r2, r3, first, second):
    total = own_in[...] + r1[...] + r2[...] + r3[...]
    first[...] = jnp.transpose(total[0:16])
    second[...] = jnp.transpose(total[16:32])


def local_call(kernel, outs, scratch=()):
    whole = pl.BlockSpec(memory_space=pltpu.VMEM)

    def call(*operands):
        return pl.pallas_call(
            kernel,
            out_shape=[jax.ShapeDtypeStruct(shape, kind) for shape, kind in outs],
            in_specs=[whole] * len(operands),
            out_specs=[whole] * len(outs),
            scratch_shapes=list(scratch),
            compiler_params=pltpu.CompilerParams(vmem_limit_bytes=60 * 1024 * 1024),
        )(*operands)

    return call


def summed(send, keep):
    got = moved(send, lambda z, yl, x, yh, core: (z, yl, x, yh, 1 - core))
    size = (2, 16, 2 * TAPS)
    own, s1, s2, s3 = local_call(after_core_kernel, [(size, F32)] + [(size, BF16)] * 3)(keep, got)
    r1, r2, r3 = [
        moved(s, lambda z, yl, x, yh, core, k=k: (z, yl, (x + k) % 4, yh, core)) for k, s in ((1, s1), (2, s2), (3, s3))
    ]
    size = (8, 32, 144)
    own, s1, s2, s3 = local_call(
        after_x_kernel, [(size, F32)] + [(size, BF16)] * 3, [pltpu.VMEM((2, 2) + size, F32)]
    )(own, r1, r2, r3)
    r1 = moved(s1, lambda z, yl, x, yh, core: (z, 1 - yl, x, yh, core))
    r2 = moved(s2, lambda z, yl, x, yh, core: (z, yl, x, 1 - yh, core))
    r3 = moved(s3, lambda z, yl, x, yh, core: (z, 1 - yl, x, 1 - yh, core))
    size = (4, 32, 144)
    own, s1 = local_call(after_y_kernel, [(size, F32)] * 2)(own, r1, r2, r3)
    r1 = moved(s1, lambda z, yl, x, yh, core: (z ^ 1, yl, x, yh, core))
    size = (32, 144)
    own, s1, s2, s3 = local_call(after_pair_kernel, [(size, F32)] * 4)(own, r1)
    r1, r2, r3 = [
        moved(s, lambda z, yl, x, yh, core, k=k: ((z + 2 * k) % 8, yl, x, yh, core)) for k, s in ((1, s1), (2, s2), (3, s3))
    ]
    return local_call(last_kernel, [((144, 16), F32)] * 2)(own, r1, r2, r3)


def turned_weight(weight):
    return weight[::-1, ::-1].transpose(0, 1, 3, 2).reshape(TAPS, C)


def on_device(latent, w_first, w_second, levels, prior_scale, bins, code_grad):
    lon, lat = lon_lat()
    low = lon < 8

    def edge(last):
        start = jnp.where(last, ROWS, 0)
        four = lax.dynamic_slice_in_dim(latent, jnp.where(last, ROWS - 4, 0), 4, 0)
        code = lax.dynamic_slice_in_dim(code_grad, jnp.where(last, ROWS - 2, 0), 2, 0)
        bin_rows = lax.dynamic_slice_in_dim(bins, jnp.where(last, ROWS - 2, 0), 2, 0).astype(BF16)
        return jnp.concatenate([four, code, bin_rows], axis=0)

    cw = lax.ppermute(edge(low), ("lon", "lat"), ring_pairs(1))
    ccw = lax.ppermute(edge(jnp.logical_not(low)), ("lon", "lat"), ring_pairs(-1))
    strip = ((EXT * 8, C), BF16)
    east, west = local_call(strips_kernel, [strip] * 2)(latent, code_grad, bins, cw, ccw)
    count = lax.axis_size("lon")
    from_west = lax.ppermute(east, "lon", [(i, (i + 1) % count) for i in range(count)])
    from_east = lax.ppermute(west, "lon", [((i + 1) % count, i) for i in range(count)])

    frame = pltpu.VMEM((2, N + 2 * BASE, 128), F32)
    triple = pltpu.VMEM((N, 3 * C), BF16)
    grad_latent, send, keep = local_call(
        block_kernel,
        [((ROWS, COLS, C), F32), ((8, 16, 2 * TAPS), BF16), ((8, 16, 2 * TAPS), F32)],
        [frame] * 6 + [triple] * 4 + [pltpu.VMEM((C, ROWS * COLS), BF16)],
    )(
        latent, code_grad, bins, cw, ccw, from_east, from_west,
        w_first.reshape(TAPS, C), w_second.reshape(TAPS, C), turned_weight(w_first), turned_weight(w_second),
        levels.reshape(1, C), prior_scale.reshape(1, C),
    )
    grad_first, grad_second = summed(send, keep)
    return (grad_latent, grad_first, grad_second)


def solution(mesh):
    placed = (
        P("lat", "lon", None),
        P(),
        P(),
        P(),
        P(),
        P("lat", "lon", None),
        P("lat", "lon", None),
    )
    return jax.shard_map(
        on_device,
        mesh=mesh,
        in_specs=placed,
        out_specs=(P("lat", "lon", None), P("lon", "lat"), P("lon", "lat")),
        check_vma=False,
    )
```

time: 394 us -> 113 us (0.29)
  waiting for transfers between devices: 257 us -> 38.7 us
  starting transfers between devices: 77.8 us -> 29.7 us
  Pallas kernels: 0 us -> 28.4 us
  matrix products: 14.9 us -> 0 us
  between operations: 14.4 us -> 0.74 us
  other arithmetic: 10.5 us -> 1.15 us
  local copies, waits for them, and re-layouts: 19 us -> 14 us
    unnamed x6 -> x0, waiting for transfers between devices: 150 us -> none
    reduce_scatter x2 -> x0, waiting for transfers between devices: 81.3 us -> none  [reduce_grads(): lax.psum_scatter(grads, 'lon', scatter_dimension=0, tiled=True)]
    ppermute x24 -> x15, starting transfers between devices: 77.7 us -> 29.7 us  [the longest x11 17.1 us: moved(): return lax.ppermute(block, ('lon', 'lat'), pairs)]
    pallas_call x0 -> x7, Pallas kernels: none -> 28.4 us  [call(): pl.pallas_call(kernel, out_shape=[jax.ShapeDtypeStruct(shape, kind) for s...]
    dot_general x6 -> x0, matrix products: 14.9 us -> none  [the longest x2 8.21 us: weight_grad(): lax.dot_general(patches, grad, (((0, 1), (0, 1)), ((), ())), preferred_el...]
    ppermute x24 -> x15, waiting for transfers between devices: 25.7 us -> 38.7 us  [the longest x11 31.1 us: moved(): return lax.ppermute(block, ('lon', 'lat'), pairs)]
    slice x9 -> x0, local copies, waits for them, and re-layouts: 5.01 us -> none  [the longest x2 3.64 us: transpose_return(): piece = tap_terms[:, :, slot * channels:(slot + 1) * channels]]
    add x5 -> x0, other arithmetic: 4.31 us -> none  [the longest x2 4.04 us: transpose_return(): padded + jnp.pad(piece, ((row_off, 2 - row_off), (col_off, 2 - col_off),...]
  transfers between devices with their start and end apart: 28 -> 15, of which waited for: 13 -> 12; matrix products, arithmetic and copies ran while one was open for 7% -> 3% of each run, Pallas kernels for 0% -> 0%
where the time goes in v1:
time: 113 us
  waiting for transfers between devices  38.7 us (34%)
  starting transfers between devices  29.7 us (26%)
  Pallas kernels  28.4 us (25%)
  local copies, waits for them, and re-layouts  14 us (12%)
  other arithmetic  1.15 us (1%)
    ppermute x11, waiting for transfers between devices, moved(): return lax.ppermute(block, ('lon', 'lat'), pairs)  31.1 us
    pallas_call x7, Pallas kernels, call(): pl.pallas_call(kernel, out_shape=[jax.ShapeDtypeStruct(shape, kind) for s...  28.4 us
    ppermute x11, starting transfers between devices, moved(): return lax.ppermute(block, ('lon', 'lat'), pairs)  17.1 us
    unnamed x36, local copies, waits for them, and re-layouts  8.84 us
    ppermute x1, starting transfers between devices, on_device(): lax.ppermute(west, 'lon', [((i + 1) % count, i) for i in range(count)])  8.28 us
    ppermute x1, waiting for transfers between devices, on_device(): lax.ppermute(east, 'lon', [(i, (i + 1) % count) for i in range(count)])  4.41 us
    ppermute x1, starting transfers between devices, on_device(): lax.ppermute(edge(jnp.logical_not(low)), ('lon', 'lat'), ring_pairs(-1))  4.21 us
    transpose x4, local copies, waits for them, and re-layouts, turned_weight(): return weight[::-1, ::-1].transpose(0, 1, 3, 2).reshape(TAPS, C)  3.25 us
  transfers between devices with their start and end apart: 15, of which 12 were waited for; matrix products, arithmetic and copies ran while one was open for 3% of the time, Pallas kernels for 0%

profile of v1, /device:TPU:6, one launch (start us, length us, event | category | flops | bytes accessed | tf_op | source)
XLA Modules:
  0.0 112.6 jit_solution(212134143535813767)
XLA Ops:
  3.8 4.2 %collective-permute-start.1 = (bf16[8,64,256]{2,1,0:T(8,128)(2,1)S(1)}, bf16[8,64,256]{2,1,0:T(8,128)(2,1)S(1)}, u32[]{:S(2)}, u32[]{:S(2)}) collective-permute-start(bf16[8,64,256]{2,1,0:T(8,128)(2,1)S(1)} %pad_maximum_fusion.1), channel_id=1, source_target_pairs={{0,128},{1,0},{2,1},{3,2},{4,3},{5,4},{6,5},{7,6},{8,7},{9,8},{10,... | collective-permute-start | bytes 786440 | tf_op jit(solution)/shard_map/ppermute | solution.py:363
  9.7 2.3 %collective-permute-done.cw = bf16[8,64,256]{2,1,0:T(8,128)(2,1)S(1)} collective-permute-done((bf16[8,64,256]{2,1,0:T(8,128)(2,1)S(1)}, bf16[8,64,256]{2,1,0:T(8,128)(2,1)S(1)}, u32[]{:S(2)}, u32[]{:S(2)}) %collective-permute-start) | collective-permute-done | bytes 262176 | tf_op jit(solution)/shard_map/ppermute | solution.py:362
  13.4 2.4 %shard_map.94 = (bf16[192,256]{1,0:T(8,128)(2,1)}, bf16[192,256]{1,0:T(8,128)(2,1)}) custom-call(bf16[16,64,256]{2,1,0:T(8,128)(2,1)} %latent.3, bf16[16,64,256]{2,1,0:T(8,128)(2,1)} %code.3, s32[16,64,256]{2,1,0:T(8,128)} %bins.3, bf16[8,64,256]{2,1,0:T(8,128)(2,1)} %copy-done.3, bf16[8,64,256]{2,1,0:T(8,128)(2,1)} %copy-done.4), custom_call_target="tpu_custom_call" | custom-call | tf_op jit(solution)/shard_map/pallas_call | solution.py:310
  15.8 8.3 %collective-permute-start.2 = (bf16[192,256]{1,0:T(8,128)(2,1)}, bf16[192,256]{1,0:T(8,128)(2,1)S(1)}, u32[]{:S(2)}, u32[]{:S(2)}) collective-permute-start(bf16[192,256]{1,0:T(8,128)(2,1)} %get-tuple-element.24), channel_id=1, source_target_pairs={{16,0},{32,16},{48,32},{64,48},{80,64},{96,80},{112,96},{128,112},... | collective-permute-start | bytes 294920 | tf_op jit(solution)/shard_map/ppermute | solution.py:368
  26.6 4.4 %collective-permute-done.3.from_west = bf16[192,256]{1,0:T(8,128)(2,1)S(1)} collective-permute-done((bf16[192,256]{1,0:T(8,128)(2,1)}, bf16[192,256]{1,0:T(8,128)(2,1)S(1)}, u32[]{:S(2)}, u32[]{:S(2)}) %collective-permute-start.3) | collective-permute-done | bytes 98336 | tf_op jit(solution)/shard_map/ppermute | solution.py:367
  31.7 15.1 %shard_map.95 = (f32[16,64,256]{2,1,0:T(8,128)}, bf16[8,16,4608]{2,1,0:T(8,128)(2,1)}, f32[8,16,4608]{2,1,0:T(8,128)}) custom-call(bf16[16,64,256]{2,1,0:T(8,128)(2,1)} %latent.3, bf16[16,64,256]{2,1,0:T(8,128)(2,1)} %code.3, s32[16,64,256]{2,1,0:T(8,128)} %bins.3, bf16[8,64,256]{2,1,0:T(8,128)(2,1)} %copy-done.3, bf16[8,64,256]{2,1,0:T(8,128)(2,1)} %copy-done.4, ...), custom_call_target="tpu_custom_call" | custom-call | tf_op jit(solution)/shard_map/pallas_call | solution.py:310
  46.8 3.1 %collective-permute-done.4.got = bf16[8,16,4608]{2,1,0:T(8,128)(2,1)S(1)} collective-permute-done((bf16[8,16,4608]{2,1,0:T(8,128)(2,1)}, bf16[8,16,4608]{2,1,0:T(8,128)(2,1)S(1)}, u32[]{:S(2)}, u32[]{:S(2)}) %collective-permute-start.4) | collective-permute-done | bytes 1179680 | tf_op jit(solution)/shard_map/ppermute | solution.py:46
  50.9 3.3 %shard_map.96 = (f32[2,16,4608]{2,1,0:T(8,128)}, bf16[2,16,4608]{2,1,0:T(8,128)(2,1)}, bf16[2,16,4608]{2,1,0:T(8,128)(2,1)}, bf16[2,16,4608]{2,1,0:T(8,128)(2,1)}) custom-call(f32[8,16,4608]{2,1,0:T(8,128)} %get-tuple-element.27.keep, bf16[8,16,4608]{2,1,0:T(8,128)(2,1)} %copy-done.2), custom_call_target="tpu_custom_call" | custom-call | tf_op jit(solution)/shard_map/pallas_call | solution.py:310
  54.1 2.4 %collective-permute-start.5 = (bf16[2,16,4608]{2,1,0:T(8,128)(2,1)}, bf16[2,16,4608]{2,1,0:T(8,128)(2,1)S(1)}, u32[]{:S(2)}, u32[]{:S(2)}) collective-permute-start(bf16[2,16,4608]{2,1,0:T(8,128)(2,1)} %get-tuple-element.30), channel_id=1, source_target_pairs={{0,4},{1,5},{2,6},{3,7},{4,8},{5,9},{6,10},{7,11},{8,12},{9,13},{1... | collective-permute-start | bytes 884744 | tf_op jit(solution)/shard_map/ppermute | solution.py:46
  57.4 12.4 %collective-permute-done.5.r1 = bf16[2,16,4608]{2,1,0:T(8,128)(2,1)S(1)} collective-permute-done((bf16[2,16,4608]{2,1,0:T(8,128)(2,1)}, bf16[2,16,4608]{2,1,0:T(8,128)(2,1)S(1)}, u32[]{:S(2)}, u32[]{:S(2)}) %collective-permute-start.5) | collective-permute-done | bytes 294944 | tf_op jit(solution)/shard_map/ppermute | solution.py:46
  69.8 3.3 %collective-permute-done.7.r3 = bf16[2,16,4608]{2,1,0:T(8,128)(2,1)S(1)} collective-permute-done((bf16[2,16,4608]{2,1,0:T(8,128)(2,1)}, bf16[2,16,4608]{2,1,0:T(8,128)(2,1)S(1)}, u32[]{:S(2)}, u32[]{:S(2)}) %collective-permute-start.7) | collective-permute-done | bytes 294944 | tf_op jit(solution)/shard_map/ppermute | solution.py:46
  73.8 2.5 %shard_map.97 = (f32[8,32,144]{2,1,0:T(8,128)}, bf16[8,32,144]{2,1,0:T(8,128)(2,1)}, bf16[8,32,144]{2,1,0:T(8,128)(2,1)}, bf16[8,32,144]{2,1,0:T(8,128)(2,1)}) custom-call(f32[2,16,4608]{2,1,0:T(8,128)} %get-tuple-element.29.own_in, bf16[2,16,4608]{2,1,0:T(8,128)(2,1)} %copy-done.5, bf16[2,16,4608]{2,1,0:T(8,128)(2,1)} %copy-done.6, ...), custom_call_target="tpu_custom_call" | custom-call | tf_op jit(solution)/shard_map/pallas_call | solution.py:310
  76.3 1.8 %collective-permute-start.9 = (bf16[8,32,144]{2,1,0:T(8,128)(2,1)}, bf16[8,32,144]{2,1,0:T(8,128)(2,1)S(1)}, u32[]{:S(2)}, u32[]{:S(2)}) collective-permute-start(bf16[8,32,144]{2,1,0:T(8,128)(2,1)} %get-tuple-element.35), channel_id=1, source_target_pairs={{0,2},{1,3},{2,0},{3,1},{4,6},{5,7},{6,4},{7,5},{8,10},{9,11},{10,... | collective-permute-start | bytes 221192 | tf_op jit(solution)/shard_map/ppermute | solution.py:46
  78.1 2.9 %collective-permute-start.10 = (bf16[8,32,144]{2,1,0:T(8,128)(2,1)}, bf16[8,32,144]{2,1,0:T(8,128)(2,1)S(1)}, u32[]{:S(2)}, u32[]{:S(2)}) collective-permute-start(bf16[8,32,144]{2,1,0:T(8,128)(2,1)} %get-tuple-element.36), channel_id=1, source_target_pairs={{0,18},{1,19},{2,16},{3,17},{4,22},{5,23},{6,20},{7,21},{8,26},{9,... | collective-permute-start | bytes 221192 | tf_op jit(solution)/shard_map/ppermute | solution.py:46
  81.0 1.9 %collective-permute-done.8.r1 = bf16[8,32,144]{2,1,0:T(8,128)(2,1)S(1)} collective-permute-done((bf16[8,32,144]{2,1,0:T(8,128)(2,1)}, bf16[8,32,144]{2,1,0:T(8,128)(2,1)S(1)}, u32[]{:S(2)}, u32[]{:S(2)}) %collective-permute-start.8) | collective-permute-done | bytes 73760 | tf_op jit(solution)/shard_map/ppermute | solution.py:46
  82.9 2.0 %collective-permute-done.9.r2 = bf16[8,32,144]{2,1,0:T(8,128)(2,1)S(1)} collective-permute-done((bf16[8,32,144]{2,1,0:T(8,128)(2,1)}, bf16[8,32,144]{2,1,0:T(8,128)(2,1)S(1)}, u32[]{:S(2)}, u32[]{:S(2)}) %collective-permute-start.9) | collective-permute-done | bytes 73760 | tf_op jit(solution)/shard_map/ppermute | solution.py:46
  84.9 2.3 %collective-permute-done.10.r3 = bf16[8,32,144]{2,1,0:T(8,128)(2,1)S(1)} collective-permute-done((bf16[8,32,144]{2,1,0:T(8,128)(2,1)}, bf16[8,32,144]{2,1,0:T(8,128)(2,1)S(1)}, u32[]{:S(2)}, u32[]{:S(2)}) %collective-permute-start.10) | collective-permute-done | bytes 73760 | tf_op jit(solution)/shard_map/ppermute | solution.py:46
  87.9 1.9 %shard_map.98 = (f32[4,32,144]{2,1,0:T(8,128)}, f32[4,32,144]{2,1,0:T(8,128)}) custom-call(f32[8,32,144]{2,1,0:T(8,128)} %get-tuple-element.33.own_in, bf16[8,32,144]{2,1,0:T(8,128)(2,1)} %copy-done.8, bf16[8,32,144]{2,1,0:T(8,128)(2,1)} %copy-done.9, bf16[8,32,144]{2,1,0:T(8,128)(2,1)} %copy-done.10), custom_call_target="tpu_custom_call" | custom-call | tf_op jit(solution)/shard_map/pallas_call | solution.py:310
  90.8 4.2 %collective-permute-done.11.r1 = f32[4,32,144]{2,1,0:T(8,128)S(1)} collective-permute-done((f32[4,32,144]{2,1,0:T(8,128)}, f32[4,32,144]{2,1,0:T(8,128)S(1)}, u32[]{:S(2)}, u32[]{:S(2)}) %collective-permute-start.11) | collective-permute-done | bytes 73760 | tf_op jit(solution)/shard_map/ppermute | solution.py:46
  95.7 1.6 %shard_map.99 = (f32[32,144]{1,0:T(8,128)}, f32[32,144]{1,0:T(8,128)}, f32[32,144]{1,0:T(8,128)}, f32[32,144]{1,0:T(8,128)}) custom-call(f32[4,32,144]{2,1,0:T(8,128)} %get-tuple-element.37.own_in, f32[4,32,144]{2,1,0:T(8,128)} %copy-done.11), custom_call_target="tpu_custom_call" | custom-call | tf_op jit(solution)/shard_map/pallas_call | solution.py:310
  98.7 2.6 %collective-permute-start.13 = (f32[32,144]{1,0:T(8,128)}, f32[32,144]{1,0:T(8,128)S(1)}, u32[]{:S(2)}, u32[]{:S(2)}) collective-permute-start(f32[32,144]{1,0:T(8,128)} %get-tuple-element.41), channel_id=1, source_target_pairs={{0,128},{1,129},{2,130},{3,131},{4,132},{5,133},{6,134},{7,135},{8... | collective-permute-start | bytes 55304 | tf_op jit(solution)/shard_map/ppermute | solution.py:46
  101.3 4.1 %collective-permute-start.14 = (f32[32,144]{1,0:T(8,128)}, f32[32,144]{1,0:T(8,128)S(1)}, u32[]{:S(2)}, u32[]{:S(2)}) collective-permute-start(f32[32,144]{1,0:T(8,128)} %get-tuple-element.42), channel_id=1, source_target_pairs={{0,192},{1,193},{2,194},{3,195},{4,196},{5,197},{6,198},{7,199},{8... | collective-permute-start | bytes 55304 | tf_op jit(solution)/shard_map/ppermute | solution.py:46
  108.0 1.6 %shard_map.100 = (f32[144,16]{1,0:T(8,128)}, f32[144,16]{1,0:T(8,128)}) custom-call(f32[32,144]{1,0:T(8,128)} %get-tuple-element.39.own_in, f32[32,144]{1,0:T(8,128)} %copy-done.14, f32[32,144]{1,0:T(8,128)} %copy-done.15, f32[32,144]{1,0:T(8,128)} %copy-done.16), custom_call_target="tpu_custom_call" | custom-call | tf_op jit(solution)/shard_map/pallas_call | solution.py:310
  109.5 1.6 %copy.12 = f32[144,16]{0,1:T(8,128)} copy(f32[144,16]{1,0:T(8,128)} %get-tuple-element.46) | data formatting | bytes 18432
  (58 shorter events, 19.7 us)
Async XLA Ops:
  0.6 7.4 %copy-start = (bf16[3,3,256,256]{3,2,1,0:T(8,128)(2,1)S(1)}, bf16[3,3,256,256]{3,2,1,0:T(8,128)(2,1)}, u32[]{:S(2)}) copy-start(bf16[3,3,256,256]{3,2,1,0:T(8,128)(2,1)} %param.8) | copy-start | bytes 3538948
  3.7 8.3 %collective-permute-start = (bf16[8,64,256]{2,1,0:T(8,128)(2,1)S(1)}, bf16[8,64,256]{2,1,0:T(8,128)(2,1)S(1)}, u32[]{:S(2)}, u32[]{:S(2)}) collective-permute-start(bf16[8,64,256]{2,1,0:T(8,128)(2,1)S(1)} %pad_maximum_fusion), channel_id=1, source_target_pairs={{0,1},{1,2},{2,3},{3,4},{4,5},{5,6},{6,7},{7,8},{8,9},{9,10},{10,1... | collective-permute-start | bytes 786440 | tf_op jit(solution)/shard_map/ppermute | solution.py:362
  3.8 8.2 %collective-permute-start.1 = (bf16[8,64,256]{2,1,0:T(8,128)(2,1)S(1)}, bf16[8,64,256]{2,1,0:T(8,128)(2,1)S(1)}, u32[]{:S(2)}, u32[]{:S(2)}) collective-permute-start(bf16[8,64,256]{2,1,0:T(8,128)(2,1)S(1)} %pad_maximum_fusion.1), channel_id=1, source_target_pairs={{0,128},{1,0},{2,1},{3,2},{4,3},{5,4},{6,5},{7,6},{8,7},{9,8},{10,... | collective-permute-start | bytes 786440 | tf_op jit(solution)/shard_map/ppermute | solution.py:363
  9.7 14.5 %copy-start.1 = (bf16[3,3,256,256]{3,2,1,0:T(8,128)(2,1)S(1)}, bf16[3,3,256,256]{3,2,1,0:T(8,128)(2,1)}, u32[]{:S(2)}) copy-start(bf16[3,3,256,256]{3,2,1,0:T(8,128)(2,1)} %param.9) | copy-start | bytes 3538948
  15.8 10.8 %collective-permute-start.2 = (bf16[192,256]{1,0:T(8,128)(2,1)}, bf16[192,256]{1,0:T(8,128)(2,1)S(1)}, u32[]{:S(2)}, u32[]{:S(2)}) collective-permute-start(bf16[192,256]{1,0:T(8,128)(2,1)} %get-tuple-element.24), channel_id=1, source_target_pairs={{16,0},{32,16},{48,32},{64,48},{80,64},{96,80},{112,96},{128,112},... | collective-permute-start | bytes 294920 | tf_op jit(solution)/shard_map/ppermute | solution.py:368
  24.1 6.9 %collective-permute-start.3 = (bf16[192,256]{1,0:T(8,128)(2,1)}, bf16[192,256]{1,0:T(8,128)(2,1)S(1)}, u32[]{:S(2)}, u32[]{:S(2)}) collective-permute-start(bf16[192,256]{1,0:T(8,128)(2,1)} %get-tuple-element.25), channel_id=1, source_target_pairs={{0,16},{16,32},{32,48},{48,64},{64,80},{80,96},{96,112},{112,128},... | collective-permute-start | bytes 294920 | tf_op jit(solution)/shard_map/ppermute | solution.py:367
  26.6 4.4 %copy-start.12 = (bf16[192,256]{1,0:T(8,128)(2,1)}, bf16[192,256]{1,0:T(8,128)(2,1)S(1)}, u32[]{:S(2)}) copy-start(bf16[192,256]{1,0:T(8,128)(2,1)S(1)} %collective-permute-done.2.from_east) | copy-start | bytes 294916
  46.8 3.1 %collective-permute-start.4 = (bf16[8,16,4608]{2,1,0:T(8,128)(2,1)}, bf16[8,16,4608]{2,1,0:T(8,128)(2,1)S(1)}, u32[]{:S(2)}, u32[]{:S(2)}) collective-permute-start(bf16[8,16,4608]{2,1,0:T(8,128)(2,1)} %get-tuple-element.28), channel_id=1, source_target_pairs={{0,1},{1,0},{2,3},{3,2},{4,5},{5,4},{6,7},{7,6},{8,9},{9,8},{10,11... | collective-permute-start | bytes 3538952 | tf_op jit(solution)/shard_map/ppermute | solution.py:46
  49.8 1.0 copy-start.2
  54.1 15.7 %collective-permute-start.5 = (bf16[2,16,4608]{2,1,0:T(8,128)(2,1)}, bf16[2,16,4608]{2,1,0:T(8,128)(2,1)S(1)}, u32[]{:S(2)}, u32[]{:S(2)}) collective-permute-start(bf16[2,16,4608]{2,1,0:T(8,128)(2,1)} %get-tuple-element.30), channel_id=1, source_target_pairs={{0,4},{1,5},{2,6},{3,7},{4,8},{5,9},{6,10},{7,11},{8,12},{9,13},{1... | collective-permute-start | bytes 884744 | tf_op jit(solution)/shard_map/ppermute | solution.py:46
  56.5 13.2 %collective-permute-start.6 = (bf16[2,16,4608]{2,1,0:T(8,128)(2,1)}, bf16[2,16,4608]{2,1,0:T(8,128)(2,1)S(1)}, u32[]{:S(2)}, u32[]{:S(2)}) collective-permute-start(bf16[2,16,4608]{2,1,0:T(8,128)(2,1)} %get-tuple-element.31), channel_id=1, source_target_pairs={{0,8},{1,9},{2,10},{3,11},{4,12},{5,13},{6,14},{7,15},{8,0},{9,1},... | collective-permute-start | bytes 884744 | tf_op jit(solution)/shard_map/ppermute | solution.py:46
  56.8 16.2 %collective-permute-start.7 = (bf16[2,16,4608]{2,1,0:T(8,128)(2,1)}, bf16[2,16,4608]{2,1,0:T(8,128)(2,1)S(1)}, u32[]{:S(2)}, u32[]{:S(2)}) collective-permute-start(bf16[2,16,4608]{2,1,0:T(8,128)(2,1)} %get-tuple-element.32), channel_id=1, source_target_pairs={{0,12},{1,13},{2,14},{3,15},{4,0},{5,1},{6,2},{7,3},{8,4},{9,5},{1... | collective-permute-start | bytes 884744 | tf_op jit(solution)/shard_map/ppermute | solution.py:46
  69.8 3.3 %copy-start.5 = (bf16[2,16,4608]{2,1,0:T(8,128)(2,1)}, bf16[2,16,4608]{2,1,0:T(8,128)(2,1)S(1)}, u32[]{:S(2)}) copy-start(bf16[2,16,4608]{2,1,0:T(8,128)(2,1)S(1)} %collective-permute-done.5.r1) | copy-start | bytes 884740
  69.8 3.3 %copy-start.6 = (bf16[2,16,4608]{2,1,0:T(8,128)(2,1)}, bf16[2,16,4608]{2,1,0:T(8,128)(2,1)S(1)}, u32[]{:S(2)}) copy-start(bf16[2,16,4608]{2,1,0:T(8,128)(2,1)S(1)} %collective-permute-done.6.r2) | copy-start | bytes 884740
  76.3 6.6 %collective-permute-start.8 = (bf16[8,32,144]{2,1,0:T(8,128)(2,1)}, bf16[8,32,144]{2,1,0:T(8,128)(2,1)S(1)}, u32[]{:S(2)}, u32[]{:S(2)}) collective-permute-start(bf16[8,32,144]{2,1,0:T(8,128)(2,1)} %get-tuple-element.34), channel_id=1, source_target_pairs={{0,16},{1,17},{2,18},{3,19},{4,20},{5,21},{6,22},{7,23},{8,24},{9,... | collective-permute-start | bytes 221192 | tf_op jit(solution)/shard_map/ppermute | solution.py:46
  76.3 8.6 %collective-permute-start.9 = (bf16[8,32,144]{2,1,0:T(8,128)(2,1)}, bf16[8,32,144]{2,1,0:T(8,128)(2,1)S(1)}, u32[]{:S(2)}, u32[]{:S(2)}) collective-permute-start(bf16[8,32,144]{2,1,0:T(8,128)(2,1)} %get-tuple-element.35), channel_id=1, source_target_pairs={{0,2},{1,3},{2,0},{3,1},{4,6},{5,7},{6,4},{7,5},{8,10},{9,11},{10,... | collective-permute-start | bytes 221192 | tf_op jit(solution)/shard_map/ppermute | solution.py:46
  78.1 9.1 %collective-permute-start.10 = (bf16[8,32,144]{2,1,0:T(8,128)(2,1)}, bf16[8,32,144]{2,1,0:T(8,128)(2,1)S(1)}, u32[]{:S(2)}, u32[]{:S(2)}) collective-permute-start(bf16[8,32,144]{2,1,0:T(8,128)(2,1)} %get-tuple-element.36), channel_id=1, source_target_pairs={{0,18},{1,19},{2,16},{3,17},{4,22},{5,23},{6,20},{7,21},{8,26},{9,... | collective-permute-start | bytes 221192 | tf_op jit(solution)/shard_map/ppermute | solution.py:46
  82.9 4.4 %copy-start.8 = (bf16[8,32,144]{2,1,0:T(8,128)(2,1)}, bf16[8,32,144]{2,1,0:T(8,128)(2,1)S(1)}, u32[]{:S(2)}) copy-start(bf16[8,32,144]{2,1,0:T(8,128)(2,1)S(1)} %collective-permute-done.8.r1) | copy-start | bytes 221188
  84.9 2.3 %copy-start.9 = (bf16[8,32,144]{2,1,0:T(8,128)(2,1)}, bf16[8,32,144]{2,1,0:T(8,128)(2,1)S(1)}, u32[]{:S(2)}) copy-start(bf16[8,32,144]{2,1,0:T(8,128)(2,1)S(1)} %collective-permute-done.9.r2) | copy-start | bytes 221188
  89.8 5.2 %collective-permute-start.11 = (f32[4,32,144]{2,1,0:T(8,128)}, f32[4,32,144]{2,1,0:T(8,128)S(1)}, u32[]{:S(2)}, u32[]{:S(2)}) collective-permute-start(f32[4,32,144]{2,1,0:T(8,128)} %get-tuple-element.38), channel_id=1, source_target_pairs={{0,32},{1,33},{2,34},{3,35},{4,36},{5,37},{6,38},{7,39},{8,40},{9,... | collective-permute-start | bytes 221192 | tf_op jit(solution)/shard_map/ppermute | solution.py:46
  97.3 8.1 %collective-permute-start.12 = (f32[32,144]{1,0:T(8,128)}, f32[32,144]{1,0:T(8,128)S(1)}, u32[]{:S(2)}, u32[]{:S(2)}) collective-permute-start(f32[32,144]{1,0:T(8,128)} %get-tuple-element.40), channel_id=1, source_target_pairs={{0,64},{1,65},{2,66},{3,67},{4,68},{5,69},{6,70},{7,71},{8,72},{9,... | collective-permute-start | bytes 55304 | tf_op jit(solution)/shard_map/ppermute | solution.py:46
  98.7 8.0 %collective-permute-start.13 = (f32[32,144]{1,0:T(8,128)}, f32[32,144]{1,0:T(8,128)S(1)}, u32[]{:S(2)}, u32[]{:S(2)}) collective-permute-start(f32[32,144]{1,0:T(8,128)} %get-tuple-element.41), channel_id=1, source_target_pairs={{0,128},{1,129},{2,130},{3,131},{4,132},{5,133},{6,134},{7,135},{8... | collective-permute-start | bytes 55304 | tf_op jit(solution)/shard_map/ppermute | solution.py:46
  101.3 6.0 %collective-permute-start.14 = (f32[32,144]{1,0:T(8,128)}, f32[32,144]{1,0:T(8,128)S(1)}, u32[]{:S(2)}, u32[]{:S(2)}) collective-permute-start(f32[32,144]{1,0:T(8,128)} %get-tuple-element.42), channel_id=1, source_target_pairs={{0,192},{1,193},{2,194},{3,195},{4,196},{5,197},{6,198},{7,199},{8... | collective-permute-start | bytes 55304 | tf_op jit(solution)/shard_map/ppermute | solution.py:46
  105.4 1.9 %copy-start.14 = (f32[32,144]{1,0:T(8,128)}, f32[32,144]{1,0:T(8,128)S(1)}, u32[]{:S(2)}) copy-start(f32[32,144]{1,0:T(8,128)S(1)} %collective-permute-done.12.r1) | copy-start | bytes 55300
  (8 other events, 5.4 us)

commit v2 on v1

v2 whole, which is shorter than its diff:
```python
import jax
import jax.numpy as jnp
from jax import lax
from jax.experimental import pallas as pl
from jax.experimental.pallas import tpu as pltpu
from jax.sharding import Mesh
from jax.sharding import PartitionSpec as P

RATE_WEIGHT = 0.5

F32 = jnp.float32
BF16 = jnp.bfloat16

C = 256
ROWS = 16
COLS = 64
RIM = 4
EXT = ROWS + 2 * RIM
W = 80
N = EXT * W + 16
BASE = 8
TAPS = 2304


def place():
    lon = 2 * lax.axis_index("z") + lax.axis_index("yl")
    lat = 4 * lax.axis_index("x") + 2 * lax.axis_index("yh") + lax.axis_index("core")
    return lon, lat


FINE = ("z", "yl", "x", "yh", "core")


def ring_pairs(step):
    pairs = []
    for lon in range(8):
        circle = [(lon, lat) for lat in range(16)] + [(lon + 8, lat) for lat in reversed(range(16))]
        for i, (lo, la) in enumerate(circle):
            tlo, tla = circle[(i + step) % 32]
            pairs.append((lo * 16 + la, tlo * 16 + tla))
    return pairs


def slanted_pairs(step, side):
    return [(a, (b // 16 + side) % 16 * 16 + b % 16) for a, b in ring_pairs(step)]


def moved(block, route):
    pairs = []
    for lon in range(16):
        for lat in range(16):
            z, yl, x, yh, core = route(lon // 2, lon % 2, lat // 4, lat // 2 % 2, lat % 2)
            pairs.append((lon * 16 + lat, (z * 2 + yl) * 16 + x * 4 + yh * 2 + core))
    return lax.ppermute(block, FINE, pairs)


def cotangent_of(levels, prior):
    half_levels = (levels[...].astype(F32) - 1.0) / 2.0
    scale = prior[...]
    double = 2.0 * scale
    weight = RATE_WEIGHT * half_levels

    def cotangent(code_part, bins_part):
        slope = jnp.tanh((bins_part - half_levels) / double) / scale
        return code_part + weight * slope

    return cotangent


def fetched(pairs, arrived):
    copies = [pltpu.make_async_copy(far, near, arrived.at[i]) for i, (far, near) in enumerate(pairs)]
    for copy in copies:
        copy.start()
    return copies


def rims_kernel(
    latent_far, code_far, bins_far, levels_far, prior_far,
    cw, ccw, east, west, cw_east, cw_west, ccw_east, ccw_west,
    latent, code, bins, levels, prior, arrived,
):
    pairs = (
        (latent_far, latent), (code_far, code), (bins_far, bins), (levels_far, levels), (prior_far, prior),
    )
    for copy in fetched(pairs, arrived):
        copy.wait()
    lon, lat = place()
    low = lon < 8
    cotangent = cotangent_of(levels, prior)

    def outward(k, first, last):
        cw[k] = jnp.where(low, last, first).astype(BF16)
        ccw[k] = jnp.where(low, first, last).astype(BF16)

    for k in range(4):
        outward(k, latent[k].astype(F32), latent[12 + k].astype(F32))
    for k in range(2):
        outward(
            4 + k,
            cotangent(code[k].astype(F32), bins[k].astype(F32)),
            cotangent(code[14 + k].astype(F32), bins[14 + k].astype(F32)),
        )

    spot = lax.broadcasted_iota(jnp.int32, (ROWS * 8, C), 0) % 8
    for out, cw_out, ccw_out, right in ((east, cw_east, ccw_east, True), (west, cw_west, ccw_west, False)):
        tile = slice(48, 64) if right else slice(0, 16)
        side = slice(8, 16) if right else slice(0, 8)
        x = latent[:, tile, :].astype(F32)[:, side].reshape(ROWS * 8, C)
        q = cotangent(
            code[:, tile, :].astype(F32)[:, side].reshape(ROWS * 8, C),
            bins[:, tile, :].astype(F32)[:, side].reshape(ROWS * 8, C),
        )
        if right:
            x = pltpu.roll(x, ROWS * 8 - 4, 0)
            q = pltpu.roll(q, ROWS * 8 - 2, 0)
        else:
            q = pltpu.roll(q, 4, 0)
        both = jnp.where(spot < 4, x, q)
        out[...] = both.astype(BF16)
        first, last = both[:32], both[96:]
        cw_out[...] = jnp.where(low, last, first).astype(BF16)
        ccw_out[...] = jnp.where(low, first, last).astype(BF16)


def facing(first, second, low, rows, count, mirrored):
    picked = []
    for k in range(count):
        at = rows + jnp.where(mirrored, count - 1 - k, k)
        picked.append(jnp.where(low, first[at].astype(F32), second[at].astype(F32)))
    return picked


def put(ref, at, value):
    rows = value.shape[0]
    ref[0, BASE + at : BASE + at + rows, :] = value[:, :128]
    ref[1, BASE + at : BASE + at + rows, :] = value[:, 128:]


def get(ref, at, rows):
    return jnp.concatenate([ref[0, BASE + at : BASE + at + rows, :], ref[1, BASE + at : BASE + at + rows, :]], axis=1)


def spread(dest, ref, start, stop):
    for at in range(start, stop, 320):
        rows = min(320, stop - at)
        for b in range(3):
            for half in range(2):
                lane = b * 256 + half * 128
                dest[at : at + rows, lane : lane + 128] = ref[half, pl.ds(BASE + at + b - 1, rows), :].astype(BF16)


def block_kernel(*refs):
    fars = refs[:15]
    grad_latent, send, keep = refs[15:18]
    nears = refs[18:33]
    x32, q32, a32, g32, dact, lat3, act3, go3, gp3, turn, arrived = refs[33:]
    fetches = fetched(tuple(zip(fars, nears)), arrived)
    latent, code, bins, w1, cw, ccw, from_east, from_west, cw_east, cw_west, ccw_east, ccw_west, levels, prior, w2 = nears
    p32 = a32
    for fetch in fetches[:3] + fetches[4:14]:
        fetch.wait()
    lon, lat = place()
    low = lon < 8
    at_north = lat == 0
    at_south = lat == 15
    core = lat % 2
    cotangent = cotangent_of(levels, prior)

    north = facing(cw, ccw, low, 0, 4, at_north)
    south = facing(ccw, cw, low, 0, 4, at_south)
    for k in range(4):
        put(x32, k * W + 16, north[k])
        put(x32, (20 + k) * W + 16, south[k])
    for r in range(ROWS):
        put(x32, (4 + r) * W + 16, latent[r].astype(F32))
    north_q = facing(cw, ccw, low, 4, 2, at_north)
    south_q = facing(ccw, cw, low, 4, 2, at_south)
    for k in range(2):
        put(q32, (2 + k) * W + 16, north_q[k])
        put(q32, (20 + k) * W + 16, south_q[k])
    for r in range(ROWS):
        put(q32, (4 + r) * W + 16, cotangent(code[r].astype(F32), bins[r].astype(F32)))

    rows = EXT * 8
    spot = lax.broadcasted_iota(jnp.int32, (rows, C), 0) % 8

    def column(own, cw_part, ccw_part, beside):
        side_low = beside < 8
        one, two = cw_part[...].astype(F32), ccw_part[...].astype(F32)

        def end(value, mirrored):
            tiles = [value[8 * k : 8 * k + 8] for k in range(4)]
            return jnp.where(mirrored, jnp.concatenate(tiles[::-1], axis=0), value)

        north = end(jnp.where(side_low, one, two), at_north)
        south = end(jnp.where(side_low, two, one), at_south)
        return jnp.concatenate([north, own[...].astype(F32), south], axis=0)

    left = column(from_west, cw_east, ccw_east, (lon + 15) % 16)
    right = column(from_east, cw_west, ccw_west, (lon + 1) % 16)

    def turned(value, by):
        return pltpu.roll(value, by % rows, 0)

    right_x = jnp.where(spot < 4, right, 0.0)
    left_x = jnp.where(spot >= 4, turned(left, 4), 0.0)
    right_q = jnp.where(spot < 2, turned(right, -4), 0.0)
    left_q = jnp.where(spot >= 6, turned(left, 2), 0.0)
    blank = jnp.zeros((8, C), F32)
    put(x32, -8, blank)
    put(x32, 0, blank)
    put(x32, N - 8, blank)
    put(x32, N, blank)
    for r in range(EXT):
        part = slice(r * 8, r * 8 + 8)
        put(x32, (r + 1) * W, right_x[part])
        put(x32, r * W + 8, left_x[part])
        if 2 <= r < 22:
            put(q32, (r + 1) * W, right_q[part])
            put(q32, r * W + 8, left_q[part])
    put(q32, 2 * W, blank)
    put(q32, 22 * W + 8, blank)

    def product(source, at, count, weights, order):
        total = None
        for slot in range(3):
            begin = order[slot]
            if not isinstance(begin, int):
                begin = pl.multiple_of(begin, 256)
            piece = jnp.dot(
                source[at + (slot - 1) * W : at + (slot - 1) * W + count, :],
                weights[pl.ds(begin, 768), :],
                preferred_element_type=F32,
            )
            total = piece if total is None else total + piece
        return total

    def returned(parts, weights, a):
        total = None
        for b in range(3):
            begin = (3 * a + 2 - b) * 256
            if not isinstance(begin, int):
                begin = pl.multiple_of(begin, 256)
            piece = lax.dot_general(
                parts[:, 256 * b : 256 * (b + 1)],
                weights[pl.ds(begin, 256), :],
                (((1,), (1,)), ((), ())),
                preferred_element_type=F32,
            )
            total = piece if total is None else total + piece
        return total

    plain = (0, 768, 1536)
    top_flip = (jnp.where(at_north, 1536, 0), 768, jnp.where(at_north, 0, 1536))
    low_flip = (jnp.where(at_south, 1536, 0), 768, jnp.where(at_south, 0, 1536))
    above_tap = jnp.where(at_north, 0, 2)
    below_tap = jnp.where(at_south, 2, 0)

    def pieces(first, last, top, bottom, orders, plain=plain):
        cuts = [(first, top, orders[0])]
        middle = (bottom - top) // 2
        cuts += [(top, top + middle, plain), (top + middle, bottom, plain)]
        cuts += [(bottom, last, orders[1])]
        out = []
        for i, (start, stop, order) in enumerate(cuts):
            out.append((start * W, (stop - start) * W + 16, 8 if i else 0, order))
        return out

    spread(lat3, x32, 0, N)
    fetches[3].wait()
    for at, count, skip, order in pieces(1, 23, 4, 20, (top_flip, low_flip)):
        pre = product(lat3, at, count, w1, order)[skip:]
        sig = jax.nn.sigmoid(pre)
        put(dact, at + skip, sig * (1.0 + pre * (1.0 - sig)))
        put(a32, at + skip, pre * sig)

    spread(act3, a32, W, 23 * W + 16)
    fetches[14].wait()
    for at, count, skip, order in pieces(2, 22, 4, 20, (top_flip, low_flip)):
        conv = product(act3, at, count, w2, order)[skip:]
        size = count - skip
        bounded = jnp.tanh(get(x32, at + skip, size) + conv)
        out = get(q32, at + skip, size) * (1.0 - bounded * bounded)
        put(g32, at + skip, out.astype(BF16).astype(F32))

    def own_cells(source, shift):
        return jnp.concatenate(
            [source[(r + shift) * W + 16 : (r + shift) * W + 80, :] for r in range(4, 20)], axis=0
        )

    def weight_grad(source, grad3, lane):
        turn[...] = jnp.transpose(own_cells(grad3.at[:, 256:512], 0))
        for a in range(3):
            full = jnp.dot(turn[...], own_cells(source, a - 1), preferred_element_type=F32)
            full = full.reshape(8, 2, 16, 768) * (1.0 / 512.0)
            mine = jnp.where(core == 0, full[:, 0], full[:, 1])
            other = jnp.where(core == 0, full[:, 1], full[:, 0])
            keep[:, :, lane + 768 * a : lane + 768 * (a + 1)] = mine
            send[:, :, lane + 768 * a : lane + 768 * (a + 1)] = other.astype(BF16)

    spread(go3, g32, 2 * W, 22 * W + 16)
    weight_grad(act3, go3, TAPS)

    taps = ((above_tap, 1, 0), (2, 1, below_tap))
    for at, count, skip, order in pieces(3, 21, 5, 19, taps, (2, 1, 0)):
        back = None
        for slot in range(3):
            begin = at + (slot - 1) * W
            piece = returned(go3[begin : begin + count, :], w2, order[slot])
            back = piece if back is None else back + piece
        back = back[skip:]
        grad = back * get(dact, at + skip, count - skip)
        put(p32, at + skip, grad)

    spread(gp3, p32, 3 * W, 21 * W + 16)
    weight_grad(lat3, gp3, 0)

    def rows_of(first, count):
        return jnp.concatenate([gp3[r * W + 16 : r * W + 80, :] for r in range(first, first + count)], axis=0)

    def tapped(first, count, a):
        return returned(rows_of(first, count), w1, a)

    above = jnp.concatenate([tapped(3, 1, above_tap), tapped(4, 15, 2)], axis=0)
    below = jnp.concatenate([tapped(5, 15, 0), tapped(20, 1, below_tap)], axis=0)
    total = tapped(4, 16, 1) + above + below
    for r in range(ROWS):
        grad_latent[r] = total[r * COLS : (r + 1) * COLS] + get(g32, (4 + r) * W + 16, COLS)


def after_core_kernel(keep, got, own, s1, s2, s3):
    x = lax.axis_index("x")

    def part(to):
        return keep[pl.ds(2 * to, 2)] + got[pl.ds(2 * to, 2)].astype(F32)

    own[...] = part(x)
    for k, out in ((1, s1), (2, s2), (3, s3)):
        out[...] = part((x + k) % 4).astype(BF16)


def after_x_kernel(own_in, r1, r2, r3, own, s1, s2, s3, parts):
    yl, yh = lax.axis_index("yl"), lax.axis_index("yh")
    for h in range(2):
        total = own_in[h] + r1[h].astype(F32) + r2[h].astype(F32) + r3[h].astype(F32)
        for tensor in range(2):
            for odd in range(2):
                lanes = [tensor * TAPS + 144 * (2 * z + odd) for z in range(8)]
                chosen = jnp.concatenate([total[:, lane : lane + 144] for lane in lanes], axis=1)
                parts[odd, h, 16 * tensor : 16 * tensor + 16, :] = chosen
    own[...] = parts[yl, yh]
    s1[...] = parts[1 - yl, yh].astype(BF16)
    s2[...] = parts[yl, 1 - yh].astype(BF16)
    s3[...] = parts[1 - yl, 1 - yh].astype(BF16)


def after_y_kernel(own_in, r1, r2, r3, out):
    total = own_in[...] + r1[...].astype(F32) + r2[...].astype(F32) + r3[...].astype(F32)
    for z in range(8):
        out[z] = total[:, 144 * z : 144 * z + 144].astype(BF16)


def local_call(kernel, outs, scratch=(), near=True, room=8, far_ins=(), near_outs=None):
    whole = pl.BlockSpec(memory_space=pltpu.VMEM)
    far = pl.BlockSpec(memory_space=pl.ANY)

    def call(*operands):
        if near:
            operands = [pltpu.with_memory_space_constraint(v, pltpu.VMEM) for v in operands]
        shapes = [
            pltpu.VMEM(shape, kind) if near_outs is None or i in near_outs else jax.ShapeDtypeStruct(shape, kind)
            for i, (shape, kind) in enumerate(outs)
        ]
        return pl.pallas_call(
            kernel,
            out_shape=shapes,
            in_specs=[far if i in far_ins else whole for i in range(len(operands))],
            out_specs=[whole] * len(outs),
            scratch_shapes=list(scratch),
            compiler_params=pltpu.CompilerParams(vmem_limit_bytes=room * 1024 * 1024),
        )(*operands)

    return call


def summed(send, keep):
    got = lax.ppermute(send, "core", [(0, 1), (1, 0)])
    size = (2, 16, 2 * TAPS)
    own, s1, s2, s3 = local_call(after_core_kernel, [(size, F32)] + [(size, BF16)] * 3)(keep, got)
    r1, r2, r3 = [
        moved(s, lambda z, yl, x, yh, core, k=k: (z, yl, (x + k) % 4, yh, core)) for k, s in ((1, s1), (2, s2), (3, s3))
    ]
    size = (32, TAPS // 2)
    own, s1, s2, s3 = local_call(
        after_x_kernel, [(size, F32)] + [(size, BF16)] * 3, [pltpu.VMEM((2, 2) + size, F32)]
    )(own, r1, r2, r3)
    r1 = moved(s1, lambda z, yl, x, yh, core: (z, 1 - yl, x, yh, core))
    r2 = moved(s2, lambda z, yl, x, yh, core: (z, yl, x, 1 - yh, core))
    r3 = moved(s3, lambda z, yl, x, yh, core: (z, 1 - yl, x, 1 - yh, core))
    (parts,) = local_call(after_y_kernel, [((8, 32, 144), BF16)])(own, r1, r2, r3)
    parts = lax.all_to_all(parts, "z", 0, 0)
    total = jnp.sum(parts.astype(F32), axis=0)
    return total[:16].T, total[16:].T


def on_device(latent, w_first, w_second, levels, prior_scale, bins, code_grad):
    levels = levels.reshape(1, C)
    prior = prior_scale.reshape(1, C)
    given = [pltpu.with_memory_space_constraint(v, pltpu.HBM) for v in (latent, code_grad, bins, levels, prior)]
    edge = ((6, COLS, C), BF16)
    strip = ((ROWS * 8, C), BF16)
    corner = ((32, C), BF16)
    cells = (ROWS, COLS, C)
    cw, ccw, east, west, cw_east, cw_west, ccw_east, ccw_west = local_call(
        rims_kernel,
        [edge, edge, strip, strip] + [corner] * 4,
        [pltpu.VMEM(v.shape, v.dtype) for v in given] + [pltpu.SemaphoreType.DMA((5,))],
        near=False, far_ins=range(5),
    )(*given)
    cw = lax.ppermute(cw, FINE, ring_pairs(1))
    ccw = lax.ppermute(ccw, FINE, ring_pairs(-1))
    from_west = lax.ppermute(east, ("z", "yl"), [(i, (i + 1) % 16) for i in range(16)])
    from_east = lax.ppermute(west, ("z", "yl"), [((i + 1) % 16, i) for i in range(16)])
    cw_east = lax.ppermute(cw_east, FINE, slanted_pairs(1, 1))
    cw_west = lax.ppermute(cw_west, FINE, slanted_pairs(1, -1))
    ccw_east = lax.ppermute(ccw_east, FINE, slanted_pairs(-1, 1))
    ccw_west = lax.ppermute(ccw_west, FINE, slanted_pairs(-1, -1))

    frame = pltpu.VMEM((2, N + 2 * BASE, 128), F32)
    triple = pltpu.VMEM((N, 3 * C), BF16)
    w1, w2 = [pltpu.with_memory_space_constraint(w.reshape(TAPS, C), pltpu.HBM) for w in (w_first, w_second)]
    fars = given[:3] + [w1, cw, ccw, from_east, from_west, cw_east, cw_west, ccw_east, ccw_west] + given[3:] + [w2]
    grad_latent, send, keep = local_call(
        block_kernel,
        [(cells, F32), ((8, 16, 2 * TAPS), BF16), ((8, 16, 2 * TAPS), F32)],
        [pltpu.VMEM(v.shape, v.dtype) for v in fars]
        + [frame] * 5 + [triple] * 4 + [pltpu.VMEM((C, ROWS * COLS), BF16), pltpu.SemaphoreType.DMA((15,))],
        near=False, room=44, far_ins=range(15), near_outs=(1, 2),
    )(*fars)
    grad_first, grad_second = summed(send, keep)
    return (grad_latent, grad_first, grad_second)


def solution(mesh):
    fine = Mesh(mesh.devices.reshape(8, 2, 4, 2, 2), FINE)
    lon, lat = ("z", "yl"), ("x", "yh", "core")
    placed = (P(lat, lon, None), P(), P(), P(), P(), P(lat, lon, None), P(lat, lon, None))
    return jax.shard_map(
        on_device,
        mesh=fine,
        in_specs=placed,
        out_specs=(P(lat, lon, None), P(lon, lat), P(lon, lat)),
        check_vma=False,
    )
```

time: 113 us -> 96.7 us (0.86)
  blocking collectives: 0 us -> 14.3 us
  local copies, waits for them, and re-layouts: 14 us -> 0.62 us
  Pallas kernels: 28.4 us -> 17.6 us
  starting transfers between devices: 29.7 us -> 24.5 us
    all_to_all x0 -> x1, blocking collectives: none -> 14.3 us  [summed(): parts = lax.all_to_all(parts, 'z', 0, 0)]
    pallas_call x7 -> x5, Pallas kernels: 28.4 us -> 17.6 us  [call(): pl.pallas_call(kernel, out_shape=shapes, in_specs=[far if i in far_ins el...]
    unnamed x36 -> x0, local copies, waits for them, and re-layouts: 8.84 us -> none
    ppermute x15, starting transfers between devices: 29.7 us -> 24.5 us  [the longest x6 11.5 us: moved(): return lax.ppermute(block, FINE, pairs)]
    transpose x4 -> x1, local copies, waits for them, and re-layouts: 3.25 us -> 0.62 us  [summed(): return (total[:16].T, total[16:].T)]
    dynamic_slice x2 -> x0, local copies, waits for them, and re-layouts: 1.88 us -> none  [the longest x1 1 us: edge(): four = lax.dynamic_slice_in_dim(latent, jnp.where(last, ROWS - 4, 0), 4, 0)]
  transfers between devices with their start and end apart: 15 -> 15, of which waited for: 12 -> 10; matrix products, arithmetic and copies ran while one was open for 3% -> 0% of each run, Pallas kernels for 0% -> 0%
where the time goes in v2:
time: 96.7 us; the launch traced here: 96 us
  waiting for transfers between devices  38.2 us (40%)
  starting transfers between devices  24.5 us (25%)
  Pallas kernels  17.6 us (18%)
  blocking collectives  14.3 us (15%)
    ppermute x6, waiting for transfers between devices, moved(): return lax.ppermute(block, FINE, pairs)  20.3 us
    pallas_call x5, Pallas kernels, call(): pl.pallas_call(kernel, out_shape=shapes, in_specs=[far if i in far_ins el...  17.6 us
    all_to_all x1, blocking collectives, summed(): parts = lax.all_to_all(parts, 'z', 0, 0)  14.3 us
    ppermute x6, starting transfers between devices, moved(): return lax.ppermute(block, FINE, pairs)  11.5 us
    ppermute x1, waiting for transfers between devices, on_device(): ccw_east = lax.ppermute(ccw_east, FINE, slanted_pairs(-1, 1))  8.46 us
    ppermute x1, starting transfers between devices, on_device(): lax.ppermute(west, ('z', 'yl'), [((i + 1) % 16, i) for i in range(16)])  4.72 us
    ppermute x1, starting transfers between devices, on_device(): ccw = lax.ppermute(ccw, FINE, ring_pairs(-1))  4.14 us
    ppermute x1, waiting for transfers between devices, on_device(): cw_west = lax.ppermute(cw_west, FINE, slanted_pairs(1, -1))  3.11 us
  transfers between devices with their start and end apart: 15, of which 10 were waited for; matrix products, arithmetic and copies ran while one was open for 0% of the time, Pallas kernels for 0%

profile of v2, /device:TPU:6, one launch (start us, length us, event | category | flops | bytes accessed | tf_op | source)
XLA Modules:
  0.0 96.0 jit_solution(4416563501075453553)
XLA Ops:
  0.6 1.9 %shard_map.94 = (bf16[6,64,256]{2,1,0:T(8,128)(2,1)S(1)}, bf16[6,64,256]{2,1,0:T(8,128)(2,1)S(1)}, bf16[128,256]{1,0:T(8,128)(2,1)S(1)}, bf16[128,256]{1,0:T(8,1...) custom-call(bf16[16,64,256]{2,1,0:T(8,128)(2,1)} %refs_0_.1, ...), custom_call_target="tpu_custom_call" | custom-call | tf_op jit(solution)/shard_map/pallas_call | solution.py:374
  2.6 4.1 %collective-permute-start.1 = (bf16[6,64,256]{2,1,0:T(8,128)(2,1)S(1)}, bf16[6,64,256]{2,1,0:T(8,128)(2,1)S(1)}, u32[]{:S(2)}, u32[]{:S(2)}) collective-permute-start(bf16[6,64,256]{2,1,0:T(8,128)(2,1)S(1)} %get-tuple-element.23), channel_id=1, source_target_pairs={{0,128},{1,0},{2,1},{3,2},{4,3},{5,4},{6,5},{7,6},{8,7},{9,8},{10,... | collective-permute-start | bytes 589832 | tf_op jit(solution)/shard_map/ppermute | solution.py:421
  6.7 4.7 %collective-permute-start.2 = (bf16[128,256]{1,0:T(8,128)(2,1)S(1)}, bf16[128,256]{1,0:T(8,128)(2,1)S(1)}, u32[]{:S(2)}, u32[]{:S(2)}) collective-permute-start(bf16[128,256]{1,0:T(8,128)(2,1)S(1)} %get-tuple-element.24), channel_id=1, source_target_pairs={{16,0},{32,16},{48,32},{64,48},{80,64},{96,80},{112,96},{128,112},... | collective-permute-start | bytes 196616 | tf_op jit(solution)/shard_map/ppermute | solution.py:423
  11.5 2.1 %collective-permute-done.4.refs_8_ = bf16[32,256]{1,0:T(8,128)(2,1)S(1)} collective-permute-done((bf16[32,256]{1,0:T(8,128)(2,1)S(1)}, bf16[32,256]{1,0:T(8,128)(2,1)S(1)}, u32[]{:S(2)}, u32[]{:S(2)}) %collective-permute-start.4) | collective-permute-done | bytes 16416 | tf_op jit(solution)/shard_map/ppermute | solution.py:424
  13.6 2.2 %collective-permute-start.5 = (bf16[32,256]{1,0:T(8,128)(2,1)S(1)}, bf16[32,256]{1,0:T(8,128)(2,1)S(1)}, u32[]{:S(2)}, u32[]{:S(2)}) collective-permute-start(bf16[32,256]{1,0:T(8,128)(2,1)S(1)} %get-tuple-element.27), channel_id=1, source_target_pairs={{0,241},{1,242},{2,243},{3,244},{4,245},{5,246},{6,247},{7,248},{8... | collective-permute-start | bytes 49160 | tf_op jit(solution)/shard_map/ppermute | solution.py:425
  15.7 3.1 %collective-permute-done.5.refs_9_ = bf16[32,256]{1,0:T(8,128)(2,1)S(1)} collective-permute-done((bf16[32,256]{1,0:T(8,128)(2,1)S(1)}, bf16[32,256]{1,0:T(8,128)(2,1)S(1)}, u32[]{:S(2)}, u32[]{:S(2)}) %collective-permute-start.5) | collective-permute-done | bytes 16416 | tf_op jit(solution)/shard_map/ppermute | solution.py:425
  18.8 8.5 %collective-permute-done.6.refs_10_ = bf16[32,256]{1,0:T(8,128)(2,1)S(1)} collective-permute-done((bf16[32,256]{1,0:T(8,128)(2,1)S(1)}, bf16[32,256]{1,0:T(8,128)(2,1)S(1)}, u32[]{:S(2)}, u32[]{:S(2)}) %collective-permute-start.6) | collective-permute-done | bytes 16416 | tf_op jit(solution)/shard_map/ppermute | solution.py:426
  27.3 1.7 %collective-permute-start.7 = (bf16[32,256]{1,0:T(8,128)(2,1)S(1)}, bf16[32,256]{1,0:T(8,128)(2,1)S(1)}, u32[]{:S(2)}, u32[]{:S(2)}) collective-permute-start(bf16[32,256]{1,0:T(8,128)(2,1)S(1)} %get-tuple-element.29), channel_id=1, source_target_pairs={{0,112},{1,240},{2,241},{3,242},{4,243},{5,244},{6,245},{7,246},{8... | collective-permute-start | bytes 49160 | tf_op jit(solution)/shard_map/ppermute | solution.py:427
  29.0 1.4 %collective-permute-done.7.refs_11_ = bf16[32,256]{1,0:T(8,128)(2,1)S(1)} collective-permute-done((bf16[32,256]{1,0:T(8,128)(2,1)S(1)}, bf16[32,256]{1,0:T(8,128)(2,1)S(1)}, u32[]{:S(2)}, u32[]{:S(2)}) %collective-permute-start.7) | collective-permute-done | bytes 16416 | tf_op jit(solution)/shard_map/ppermute | solution.py:427
  30.5 15.2 %shard_map.95 = (f32[16,64,256]{2,1,0:T(8,128)}, bf16[8,16,4608]{2,1,0:T(8,128)(2,1)S(1)}, f32[8,16,4608]{2,1,0:T(8,128)S(1)}) custom-call(bf16[16,64,256]{2,1,0:T(8,128)(2,1)} %refs_0_.1, bf16[16,64,256]{2,1,0:T(8,128)(2,1)} %refs_1_.1, s32[16,64,256]{2,1,0:T(8,128)} %refs_2_.1, bf16[2304,256]{1,0:T(8,128)(2,1)} %bitcast.8, ...), custom_call_target="tpu_custom_call" | custom-call | tf_op jit(solution)/shard_map/pallas_call | solution.py:374
  45.8 2.8 %collective-permute-done.8.got = bf16[8,16,4608]{2,1,0:T(8,128)(2,1)S(1)} collective-permute-done((bf16[8,16,4608]{2,1,0:T(8,128)(2,1)S(1)}, bf16[8,16,4608]{2,1,0:T(8,128)(2,1)S(1)}, u32[]{:S(2)}, u32[]{:S(2)}) %collective-permute-start.8) | collective-permute-done | bytes 1179680 | tf_op jit(solution)/shard_map/ppermute | solution.py:387
  48.6 0.2 shard_map.96
  48.8 5.8 %collective-permute-start.9 = (bf16[2,16,4608]{2,1,0:T(8,128)(2,1)S(1)}, bf16[2,16,4608]{2,1,0:T(8,128)(2,1)S(1)}, u32[]{:S(2)}, u32[]{:S(2)}) collective-permute-start(bf16[2,16,4608]{2,1,0:T(8,128)(2,1)S(1)} %get-tuple-element.34), channel_id=1, source_target_pairs={{0,4},{1,5},{2,6},{3,7},{4,8},{5,9},{6,10},{7,11},{8,12},{9,13},{1... | collective-permute-start | bytes 884744 | tf_op jit(solution)/shard_map/ppermute | solution.py:54
  54.6 1.0 collective-permute-start.11
  55.5 12.2 %collective-permute-done.9.r1 = bf16[2,16,4608]{2,1,0:T(8,128)(2,1)S(1)} collective-permute-done((bf16[2,16,4608]{2,1,0:T(8,128)(2,1)S(1)}, bf16[2,16,4608]{2,1,0:T(8,128)(2,1)S(1)}, u32[]{:S(2)}, u32[]{:S(2)}) %collective-permute-start.9) | collective-permute-done | bytes 294944 | tf_op jit(solution)/shard_map/ppermute | solution.py:54
  67.7 3.4 %collective-permute-done.11.r3 = bf16[2,16,4608]{2,1,0:T(8,128)(2,1)S(1)} collective-permute-done((bf16[2,16,4608]{2,1,0:T(8,128)(2,1)S(1)}, bf16[2,16,4608]{2,1,0:T(8,128)(2,1)S(1)}, u32[]{:S(2)}, u32[]{:S(2)}) %collective-permute-start.11) | collective-permute-done | bytes 294944 | tf_op jit(solution)/shard_map/ppermute | solution.py:54
  71.1 0.3 shard_map.97
  71.5 3.8 %collective-permute-start.13 = (bf16[32,1152]{1,0:T(8,128)(2,1)S(1)}, bf16[32,1152]{1,0:T(8,128)(2,1)S(1)}, u32[]{:S(2)}, u32[]{:S(2)}) collective-permute-start(bf16[32,1152]{1,0:T(8,128)(2,1)S(1)} %get-tuple-element.39), channel_id=1, source_target_pairs={{0,2},{1,3},{2,0},{3,1},{4,6},{5,7},{6,4},{7,5},{8,10},{9,11},{10,... | collective-permute-start | bytes 221192 | tf_op jit(solution)/shard_map/ppermute | solution.py:54
  75.4 0.9 collective-permute-start.14
  76.2 0.2 collective-permute-done.12.r1
  76.4 2.8 %collective-permute-done.13.r2 = bf16[32,1152]{1,0:T(8,128)(2,1)S(1)} collective-permute-done((bf16[32,1152]{1,0:T(8,128)(2,1)S(1)}, bf16[32,1152]{1,0:T(8,128)(2,1)S(1)}, u32[]{:S(2)}, u32[]{:S(2)}) %collective-permute-start.13) | collective-permute-done | bytes 73760 | tf_op jit(solution)/shard_map/ppermute | solution.py:54
  79.2 1.8 %collective-permute-done.14.r3 = bf16[32,1152]{1,0:T(8,128)(2,1)S(1)} collective-permute-done((bf16[32,1152]{1,0:T(8,128)(2,1)S(1)}, bf16[32,1152]{1,0:T(8,128)(2,1)S(1)}, u32[]{:S(2)}, u32[]{:S(2)}) %collective-permute-start.14) | collective-permute-done | bytes 73760 | tf_op jit(solution)/shard_map/ppermute | solution.py:54
  81.0 14.3 %all_to_all.5 = bf16[8,32,144]{2,1,0:T(8,128)(2,1)S(1)} all-to-all(bf16[8,32,144]{2,1,0:T(8,128)(2,1)S(1)} %shard_map.98), channel_id=1, replica_groups=mesh['z'=8,'yl'=2,'x'=4,'yh'=2,'core'=2] {'z'}, dimensions={0} | all-to-all | bytes 147456 | tf_op jit(solution)/shard_map/all_to_all | solution.py:401
  95.3 0.6 slice_bitcast_fusion
  (14 shorter events, 0.4 us)
Async XLA Ops:
  2.5 28.0 %collective-permute-start = (bf16[6,64,256]{2,1,0:T(8,128)(2,1)S(1)}, bf16[6,64,256]{2,1,0:T(8,128)(2,1)S(1)}, u32[]{:S(2)}, u32[]{:S(2)}) collective-permute-start(bf16[6,64,256]{2,1,0:T(8,128)(2,1)S(1)} %get-tuple-element.22), channel_id=1, source_target_pairs={{0,1},{1,2},{2,3},{3,4},{4,5},{5,6},{6,7},{7,8},{8,9},{9,10},{10,1... | collective-permute-start | bytes 589832 | tf_op jit(solution)/shard_map/ppermute | solution.py:420
  2.6 27.9 %collective-permute-start.1 = (bf16[6,64,256]{2,1,0:T(8,128)(2,1)S(1)}, bf16[6,64,256]{2,1,0:T(8,128)(2,1)S(1)}, u32[]{:S(2)}, u32[]{:S(2)}) collective-permute-start(bf16[6,64,256]{2,1,0:T(8,128)(2,1)S(1)} %get-tuple-element.23), channel_id=1, source_target_pairs={{0,128},{1,0},{2,1},{3,2},{4,3},{5,4},{6,5},{7,6},{8,7},{9,8},{10,... | collective-permute-start | bytes 589832 | tf_op jit(solution)/shard_map/ppermute | solution.py:421
  6.7 6.8 %collective-permute-start.4 = (bf16[32,256]{1,0:T(8,128)(2,1)S(1)}, bf16[32,256]{1,0:T(8,128)(2,1)S(1)}, u32[]{:S(2)}, u32[]{:S(2)}) collective-permute-start(bf16[32,256]{1,0:T(8,128)(2,1)S(1)} %get-tuple-element.26), channel_id=1, source_target_pairs={{0,17},{1,18},{2,19},{3,20},{4,21},{5,22},{6,23},{7,24},{8,25},{9,... | collective-permute-start | bytes 49160 | tf_op jit(solution)/shard_map/ppermute | solution.py:424
  6.7 23.8 %collective-permute-start.2 = (bf16[128,256]{1,0:T(8,128)(2,1)S(1)}, bf16[128,256]{1,0:T(8,128)(2,1)S(1)}, u32[]{:S(2)}, u32[]{:S(2)}) collective-permute-start(bf16[128,256]{1,0:T(8,128)(2,1)S(1)} %get-tuple-element.24), channel_id=1, source_target_pairs={{16,0},{32,16},{48,32},{64,48},{80,64},{96,80},{112,96},{128,112},... | collective-permute-start | bytes 196616 | tf_op jit(solution)/shard_map/ppermute | solution.py:423
  11.5 19.0 %collective-permute-start.3 = (bf16[128,256]{1,0:T(8,128)(2,1)S(1)}, bf16[128,256]{1,0:T(8,128)(2,1)S(1)}, u32[]{:S(2)}, u32[]{:S(2)}) collective-permute-start(bf16[128,256]{1,0:T(8,128)(2,1)S(1)} %get-tuple-element.25), channel_id=1, source_target_pairs={{0,16},{16,32},{32,48},{48,64},{64,80},{80,96},{96,112},{112,128},... | collective-permute-start | bytes 196616 | tf_op jit(solution)/shard_map/ppermute | solution.py:422
  13.6 5.3 %collective-permute-start.5 = (bf16[32,256]{1,0:T(8,128)(2,1)S(1)}, bf16[32,256]{1,0:T(8,128)(2,1)S(1)}, u32[]{:S(2)}, u32[]{:S(2)}) collective-permute-start(bf16[32,256]{1,0:T(8,128)(2,1)S(1)} %get-tuple-element.27), channel_id=1, source_target_pairs={{0,241},{1,242},{2,243},{3,244},{4,245},{5,246},{6,247},{7,248},{8... | collective-permute-start | bytes 49160 | tf_op jit(solution)/shard_map/ppermute | solution.py:425
  18.8 8.5 %collective-permute-start.6 = (bf16[32,256]{1,0:T(8,128)(2,1)S(1)}, bf16[32,256]{1,0:T(8,128)(2,1)S(1)}, u32[]{:S(2)}, u32[]{:S(2)}) collective-permute-start(bf16[32,256]{1,0:T(8,128)(2,1)S(1)} %get-tuple-element.28), channel_id=1, source_target_pairs={{0,144},{1,16},{2,17},{3,18},{4,19},{5,20},{6,21},{7,22},{8,23},{9... | collective-permute-start | bytes 49160 | tf_op jit(solution)/shard_map/ppermute | solution.py:426
  27.3 3.2 %collective-permute-start.7 = (bf16[32,256]{1,0:T(8,128)(2,1)S(1)}, bf16[32,256]{1,0:T(8,128)(2,1)S(1)}, u32[]{:S(2)}, u32[]{:S(2)}) collective-permute-start(bf16[32,256]{1,0:T(8,128)(2,1)S(1)} %get-tuple-element.29), channel_id=1, source_target_pairs={{0,112},{1,240},{2,241},{3,242},{4,243},{5,244},{6,245},{7,246},{8... | collective-permute-start | bytes 49160 | tf_op jit(solution)/shard_map/ppermute | solution.py:427
  45.7 2.9 %collective-permute-start.8 = (bf16[8,16,4608]{2,1,0:T(8,128)(2,1)S(1)}, bf16[8,16,4608]{2,1,0:T(8,128)(2,1)S(1)}, u32[]{:S(2)}, u32[]{:S(2)}) collective-permute-start(bf16[8,16,4608]{2,1,0:T(8,128)(2,1)S(1)} %get-tuple-element.32), channel_id=1, source_target_pairs={{0,1},{1,0},{2,3},{3,2},{4,5},{5,4},{6,7},{7,6},{8,9},{9,8},{10,11... | collective-permute-start | bytes 3538952 | tf_op jit(solution)/shard_map/ppermute | solution.py:387
  48.8 18.9 %collective-permute-start.9 = (bf16[2,16,4608]{2,1,0:T(8,128)(2,1)S(1)}, bf16[2,16,4608]{2,1,0:T(8,128)(2,1)S(1)}, u32[]{:S(2)}, u32[]{:S(2)}) collective-permute-start(bf16[2,16,4608]{2,1,0:T(8,128)(2,1)S(1)} %get-tuple-element.34), channel_id=1, source_target_pairs={{0,4},{1,5},{2,6},{3,7},{4,8},{5,9},{6,10},{7,11},{8,12},{9,13},{1... | collective-permute-start | bytes 884744 | tf_op jit(solution)/shard_map/ppermute | solution.py:54
  54.6 13.1 %collective-permute-start.10 = (bf16[2,16,4608]{2,1,0:T(8,128)(2,1)S(1)}, bf16[2,16,4608]{2,1,0:T(8,128)(2,1)S(1)}, u32[]{:S(2)}, u32[]{:S(2)}) collective-permute-start(bf16[2,16,4608]{2,1,0:T(8,128)(2,1)S(1)} %get-tuple-element.35), channel_id=1, source_target_pairs={{0,8},{1,9},{2,10},{3,11},{4,12},{5,13},{6,14},{7,15},{8,0},{9,1},... | collective-permute-start | bytes 884744 | tf_op jit(solution)/shard_map/ppermute | solution.py:54
  54.6 16.5 %collective-permute-start.11 = (bf16[2,16,4608]{2,1,0:T(8,128)(2,1)S(1)}, bf16[2,16,4608]{2,1,0:T(8,128)(2,1)S(1)}, u32[]{:S(2)}, u32[]{:S(2)}) collective-permute-start(bf16[2,16,4608]{2,1,0:T(8,128)(2,1)S(1)} %get-tuple-element.36), channel_id=1, source_target_pairs={{0,12},{1,13},{2,14},{3,15},{4,0},{5,1},{6,2},{7,3},{8,4},{9,5},{1... | collective-permute-start | bytes 884744 | tf_op jit(solution)/shard_map/ppermute | solution.py:54
  71.4 5.0 %collective-permute-start.12 = (bf16[32,1152]{1,0:T(8,128)(2,1)S(1)}, bf16[32,1152]{1,0:T(8,128)(2,1)S(1)}, u32[]{:S(2)}, u32[]{:S(2)}) collective-permute-start(bf16[32,1152]{1,0:T(8,128)(2,1)S(1)} %get-tuple-element.38), channel_id=1, source_target_pairs={{0,16},{1,17},{2,18},{3,19},{4,20},{5,21},{6,22},{7,23},{8,24},{9,... | collective-permute-start | bytes 221192 | tf_op jit(solution)/shard_map/ppermute | solution.py:54
  71.5 7.6 %collective-permute-start.13 = (bf16[32,1152]{1,0:T(8,128)(2,1)S(1)}, bf16[32,1152]{1,0:T(8,128)(2,1)S(1)}, u32[]{:S(2)}, u32[]{:S(2)}) collective-permute-start(bf16[32,1152]{1,0:T(8,128)(2,1)S(1)} %get-tuple-element.39), channel_id=1, source_target_pairs={{0,2},{1,3},{2,0},{3,1},{4,6},{5,7},{6,4},{7,5},{8,10},{9,11},{10,... | collective-permute-start | bytes 221192 | tf_op jit(solution)/shard_map/ppermute | solution.py:54
  75.4 5.6 %collective-permute-start.14 = (bf16[32,1152]{1,0:T(8,128)(2,1)S(1)}, bf16[32,1152]{1,0:T(8,128)(2,1)S(1)}, u32[]{:S(2)}, u32[]{:S(2)}) collective-permute-start(bf16[32,1152]{1,0:T(8,128)(2,1)S(1)} %get-tuple-element.40), channel_id=1, source_target_pairs={{0,18},{1,19},{2,16},{3,17},{4,22},{5,23},{6,20},{7,21},{8,26},{9,... | collective-permute-start | bytes 221192 | tf_op jit(solution)/shard_map/ppermute | solution.py:54

commit v3 on v2

--- a/solution.py
+++ b/solution.py
@@ -41,10 +41,6 @@
     return pairs
 
 
-def slanted_pairs(step, side):
-    return [(a, (b // 16 + side) % 16 * 16 + b % 16) for a, b in ring_pairs(step)]
-
-
 def moved(block, route):
     pairs = []
     for lon in range(16):
@@ -76,7 +72,7 @@
 
 def rims_kernel(
     latent_far, code_far, bins_far, levels_far, prior_far,
-    cw, ccw, east, west, cw_east, cw_west, ccw_east, ccw_west,
+    cw, ccw, east, west,
     latent, code, bins, levels, prior, arrived,
 ):
     pairs = (
@@ -102,7 +98,7 @@
         )
 
     spot = lax.broadcasted_iota(jnp.int32, (ROWS * 8, C), 0) % 8
-    for out, cw_out, ccw_out, right in ((east, cw_east, ccw_east, True), (west, cw_west, ccw_west, False)):
+    for out, right in ((east, True), (west, False)):
         tile = slice(48, 64) if right else slice(0, 16)
         side = slice(8, 16) if right else slice(0, 8)
         x = latent[:, tile, :].astype(F32)[:, side].reshape(ROWS * 8, C)
@@ -115,11 +111,16 @@
             q = pltpu.roll(q, ROWS * 8 - 2, 0)
         else:
             q = pltpu.roll(q, 4, 0)
-        both = jnp.where(spot < 4, x, q)
-        out[...] = both.astype(BF16)
-        first, last = both[:32], both[96:]
-        cw_out[...] = jnp.where(low, last, first).astype(BF16)
-        ccw_out[...] = jnp.where(low, first, last).astype(BF16)
+        out[...] = jnp.where(spot < 4, x, q).astype(BF16)
+
+
+def corners_kernel(from_west, from_east, cw_corner, ccw_corner):
+    lon, lat = place()
+    low = lon < 8
+    for side, strip in enumerate((from_west, from_east)):
+        first, last = strip[0:32, :].astype(F32), strip[96:128, :].astype(F32)
+        cw_corner[32 * side : 32 * side + 32, :] = jnp.where(low, last, first).astype(BF16)
+        ccw_corner[32 * side : 32 * side + 32, :] = jnp.where(low, first, last).astype(BF16)
 
 
 def facing(first, second, low, rows, count, mirrored):
@@ -150,14 +151,14 @@
 
 
 def block_kernel(*refs):
-    fars = refs[:15]
-    grad_latent, send, keep = refs[15:18]
-    nears = refs[18:33]
-    x32, q32, a32, g32, dact, lat3, act3, go3, gp3, turn, arrived = refs[33:]
+    fars = refs[:13]
+    grad_latent, send, keep = refs[13:16]
+    nears = refs[16:29]
+    x32, q32, a32, g32, dact, lat3, act3, go3, gp3, turn, arrived = refs[29:]
     fetches = fetched(tuple(zip(fars, nears)), arrived)
-    latent, code, bins, w1, cw, ccw, from_east, from_west, cw_east, cw_west, ccw_east, ccw_west, levels, prior, w2 = nears
+    latent, code, bins, w1, cw, ccw, from_east, from_west, cw_corner, ccw_corner, levels, prior, w2 = nears
     p32 = a32
-    for fetch in fetches[:3] + fetches[4:14]:
+    for fetch in fetches[:3] + fetches[4:12]:
         fetch.wait()
     lon, lat = place()
     low = lon < 8
@@ -184,20 +185,20 @@
     rows = EXT * 8
     spot = lax.broadcasted_iota(jnp.int32, (rows, C), 0) % 8
 
-    def column(own, cw_part, ccw_part, beside):
-        side_low = beside < 8
-        one, two = cw_part[...].astype(F32), ccw_part[...].astype(F32)
+    def column(own, side):
+        one = cw_corner[32 * side : 32 * side + 32, :].astype(F32)
+        two = ccw_corner[32 * side : 32 * side + 32, :].astype(F32)
 
         def end(value, mirrored):
             tiles = [value[8 * k : 8 * k + 8] for k in range(4)]
             return jnp.where(mirrored, jnp.concatenate(tiles[::-1], axis=0), value)
 
-        north = end(jnp.where(side_low, one, two), at_north)
-        south = end(jnp.where(side_low, two, one), at_south)
+        north = end(jnp.where(low, one, two), at_north)
+        south = end(jnp.where(low, two, one), at_south)
         return jnp.concatenate([north, own[...].astype(F32), south], axis=0)
 
-    left = column(from_west, cw_east, ccw_east, (lon + 15) % 16)
-    right = column(from_east, cw_west, ccw_west, (lon + 1) % 16)
+    left = column(from_west, 0)
+    right = column(from_east, 1)
 
     def turned(value, by):
         return pltpu.roll(value, by % rows, 0)
@@ -275,7 +276,7 @@
         put(a32, at + skip, pre * sig)
 
     spread(act3, a32, W, 23 * W + 16)
-    fetches[14].wait()
+    fetches[12].wait()
     for at, count, skip, order in pieces(2, 22, 4, 20, (top_flip, low_flip)):
         conv = product(act3, at, count, w2, order)[skip:]
         size = count - skip
@@ -409,33 +410,32 @@
     given = [pltpu.with_memory_space_constraint(v, pltpu.HBM) for v in (latent, code_grad, bins, levels, prior)]
     edge = ((6, COLS, C), BF16)
     strip = ((ROWS * 8, C), BF16)
-    corner = ((32, C), BF16)
+    corner = ((64, C), BF16)
     cells = (ROWS, COLS, C)
-    cw, ccw, east, west, cw_east, cw_west, ccw_east, ccw_west = local_call(
+    cw, ccw, east, west = local_call(
         rims_kernel,
-        [edge, edge, strip, strip] + [corner] * 4,
+        [edge, edge, strip, strip],
         [pltpu.VMEM(v.shape, v.dtype) for v in given] + [pltpu.SemaphoreType.DMA((5,))],
         near=False, far_ins=range(5),
     )(*given)
+    from_west = lax.ppermute(east, ("z", "yl"), [(i, (i + 1) % 16) for i in range(16)])
+    from_east = lax.ppermute(west, ("z", "yl"), [((i + 1) % 16, i) for i in range(16)])
     cw = lax.ppermute(cw, FINE, ring_pairs(1))
     ccw = lax.ppermute(ccw, FINE, ring_pairs(-1))
-    from_west = lax.ppermute(east, ("z", "yl"), [(i, (i + 1) % 16) for i in range(16)])
-    from_east = lax.ppermute(west, ("z", "yl"), [((i + 1) % 16, i) for i in range(16)])
-    cw_east = lax.ppermute(cw_east, FINE, slanted_pairs(1, 1))
-    cw_west = lax.ppermute(cw_west, FINE, slanted_pairs(1, -1))
-    ccw_east = lax.ppermute(ccw_east, FINE, slanted_pairs(-1, 1))
-    ccw_west = lax.ppermute(ccw_west, FINE, slanted_pairs(-1, -1))
+    cw_corner, ccw_corner = local_call(corners_kernel, [corner] * 2)(from_west, from_east)
+    cw_corner = lax.ppermute(cw_corner, FINE, ring_pairs(1))
+    ccw_corner = lax.ppermute(ccw_corner, FINE, ring_pairs(-1))
 
     frame = pltpu.VMEM((2, N + 2 * BASE, 128), F32)
     triple = pltpu.VMEM((N, 3 * C), BF16)
     w1, w2 = [pltpu.with_memory_space_constraint(w.reshape(TAPS, C), pltpu.HBM) for w in (w_first, w_second)]
-    fars = given[:3] + [w1, cw, ccw, from_east, from_west, cw_east, cw_west, ccw_east, ccw_west] + given[3:] + [w2]
+    fars = given[:3] + [w1, cw, ccw, from_east, from_west, cw_corner, ccw_corner] + given[3:] + [w2]
     grad_latent, send, keep = local_call(
         block_kernel,
         [(cells, F32), ((8, 16, 2 * TAPS), BF16), ((8, 16, 2 * TAPS), F32)],
         [pltpu.VMEM(v.shape, v.dtype) for v in fars]
-        + [frame] * 5 + [triple] * 4 + [pltpu.VMEM((C, ROWS * COLS), BF16), pltpu.SemaphoreType.DMA((15,))],
-        near=False, room=44, far_ins=range(15), near_outs=(1, 2),
+        + [frame] * 5 + [triple] * 4 + [pltpu.VMEM((C, ROWS * COLS), BF16), pltpu.SemaphoreType.DMA((13,))],
+        near=False, room=44, far_ins=range(13), near_outs=(1, 2),
     )(*fars)
     grad_first, grad_second = summed(send, keep)
     return (grad_latent, grad_first, grad_second)

time: 96.7 us -> 86.5 us (0.89)
  waiting for transfers between devices: 38.2 us -> 31.4 us
  blocking collectives: 14.3 us -> 11.7 us
    ppermute x4 -> x2, waiting for transfers between devices: 15.1 us -> 2.39 us  [the longest x1 1.59 us: on_device(): cw_corner = lax.ppermute(cw_corner, FINE, ring_pairs(1))]
    ppermute x6, starting transfers between devices: 11.5 us -> 6.88 us  [moved(): return lax.ppermute(block, FINE, pairs)]
    ppermute x1, waiting for transfers between devices: 0.01 us -> 4.61 us  [on_device(): lax.ppermute(east, ('z', 'yl'), [(i, (i + 1) % 16) for i in range(16)])]
    ppermute x1, starting transfers between devices: 0.09 us -> 4.23 us  [summed(): got = lax.ppermute(send, 'core', [(0, 1), (1, 0)])]
    all_to_all x1, blocking collectives: 14.3 us -> 11.7 us  [summed(): parts = lax.all_to_all(parts, 'z', 0, 0)]
    ppermute x1, waiting for transfers between devices: 0.01 us -> 2.37 us  [on_device(): lax.ppermute(west, ('z', 'yl'), [((i + 1) % 16, i) for i in range(16)])]
    ppermute x4 -> x2, starting transfers between devices: 3.91 us -> 4.22 us  [the longest x1 4.14 us: on_device(): ccw_corner = lax.ppermute(ccw_corner, FINE, ring_pairs(-1))]
    pallas_call x5 -> x6, Pallas kernels: 17.6 us -> 17.6 us  [call(): pl.pallas_call(kernel, out_shape=shapes, in_specs=[far if i in far_ins el...]
  transfers between devices with their start and end apart: 15 -> 13, of which waited for: 10 -> 11; matrix products, arithmetic and copies ran while one was open for 0% -> 0% of each run, Pallas kernels for 0% -> 0%
where the time goes in v3:
time: 86.5 us; the launch traced here: 86.4 us
  waiting for transfers between devices  31.4 us (36%)
  starting transfers between devices  24.3 us (28%)
  Pallas kernels  17.6 us (20%)
  blocking collectives  11.7 us (14%)
    ppermute x6, waiting for transfers between devices, moved(): return lax.ppermute(block, FINE, pairs)  19.5 us
    pallas_call x6, Pallas kernels, call(): pl.pallas_call(kernel, out_shape=shapes, in_specs=[far if i in far_ins el...  17.6 us
    all_to_all x1, blocking collectives, summed(): parts = lax.all_to_all(parts, 'z', 0, 0)  11.7 us
    ppermute x6, starting transfers between devices, moved(): return lax.ppermute(block, FINE, pairs)  6.88 us
    ppermute x1, starting transfers between devices, on_device(): lax.ppermute(west, ('z', 'yl'), [((i + 1) % 16, i) for i in range(16)])  4.72 us
    ppermute x1, waiting for transfers between devices, on_device(): lax.ppermute(east, ('z', 'yl'), [(i, (i + 1) % 16) for i in range(16)])  4.61 us
    ppermute x1, starting transfers between devices, summed(): got = lax.ppermute(send, 'core', [(0, 1), (1, 0)])  4.23 us
    ppermute x1, starting transfers between devices, on_device(): ccw_corner = lax.ppermute(ccw_corner, FINE, ring_pairs(-1))  4.14 us
  transfers between devices with their start and end apart: 13, of which 11 were waited for; matrix products, arithmetic and copies ran while one was open for 0% of the time, Pallas kernels for 0%

profile of v3, /device:TPU:6, one launch (start us, length us, event | category | flops | bytes accessed | tf_op | source)
XLA Modules:
  0.0 86.4 jit_solution(14187344419228158029)
XLA Ops:
  0.6 1.9 %shard_map.94 = (bf16[6,64,256]{2,1,0:T(8,128)(2,1)S(1)}, bf16[6,64,256]{2,1,0:T(8,128)(2,1)S(1)}, bf16[128,256]{1,0:T(8,128)(2,1)S(1)}, bf16[128,256]{1,0:T(8,128)(2,1)S(1)}) custom-call(bf16[16,64,256]{2,1,0:T(8,128)(2,1)} %refs_0_.1, bf16[16,64,256]{2,1,0:T(8,128)(2,1)} %refs_1_.1, s32[16,64,256]{2,1,0:T(8,128)} %refs_2_.1, s32[1,256]{1,0:T(1,128)} %bitcast.10, ...), custom_call_target="tpu_custom_call" | custom-call | tf_op jit(solution)/shard_map/pallas_call | solution.py:375
  2.6 4.1 %collective-permute-start.1 = (bf16[6,64,256]{2,1,0:T(8,128)(2,1)S(1)}, bf16[6,64,256]{2,1,0:T(8,128)(2,1)S(1)}, u32[]{:S(2)}, u32[]{:S(2)}) collective-permute-start(bf16[6,64,256]{2,1,0:T(8,128)(2,1)S(1)} %get-tuple-element.21), channel_id=1, source_target_pairs={{0,128},{1,0},{2,1},{3,2},{4,3},{5,4},{6,5},{7,6},{8,7},{9,8},{10,... | collective-permute-start | bytes 589832 | tf_op jit(solution)/shard_map/ppermute | solution.py:424
  6.7 4.7 %collective-permute-start.2 = (bf16[128,256]{1,0:T(8,128)(2,1)S(1)}, bf16[128,256]{1,0:T(8,128)(2,1)S(1)}, u32[]{:S(2)}, u32[]{:S(2)}) collective-permute-start(bf16[128,256]{1,0:T(8,128)(2,1)S(1)} %get-tuple-element.22), channel_id=1, source_target_pairs={{16,0},{32,16},{48,32},{64,48},{80,64},{96,80},{112,96},{128,112},... | collective-permute-start | bytes 196616 | tf_op jit(solution)/shard_map/ppermute | solution.py:422
  11.4 2.4 %collective-permute-done.2.from_east.refs_6_ = bf16[128,256]{1,0:T(8,128)(2,1)S(1)} collective-permute-done((bf16[128,256]{1,0:T(8,128)(2,1)S(1)}, bf16[128,256]{1,0:T(8,128)(2,1)S(1)}, u32[]{:S(2)}, u32[]{:S(2)}) %collective-permute-start.2) | collective-permute-done | bytes 65568 | tf_op jit(solution)/shard_map/ppermute | solution.py:422
  13.8 4.6 %collective-permute-done.3.from_west.refs_7_ = bf16[128,256]{1,0:T(8,128)(2,1)S(1)} collective-permute-done((bf16[128,256]{1,0:T(8,128)(2,1)S(1)}, bf16[128,256]{1,0:T(8,128)(2,1)S(1)}, u32[]{:S(2)}, u32[]{:S(2)}) %collective-permute-start.3) | collective-permute-done | bytes 65568 | tf_op jit(solution)/shard_map/ppermute | solution.py:421
  18.5 4.1 %collective-permute-start.5 = (bf16[64,256]{1,0:T(8,128)(2,1)S(1)}, bf16[64,256]{1,0:T(8,128)(2,1)S(1)}, u32[]{:S(2)}, u32[]{:S(2)}) collective-permute-start(bf16[64,256]{1,0:T(8,128)(2,1)S(1)} %get-tuple-element.25), channel_id=1, source_target_pairs={{0,128},{1,0},{2,1},{3,2},{4,3},{5,4},{6,5},{7,6},{8,7},{9,8},{10,... | collective-permute-start | bytes 98312 | tf_op jit(solution)/shard_map/ppermute | solution.py:427
  22.7 1.6 %collective-permute-done.4.refs_8_ = bf16[64,256]{1,0:T(8,128)(2,1)S(1)} collective-permute-done((bf16[64,256]{1,0:T(8,128)(2,1)S(1)}, bf16[64,256]{1,0:T(8,128)(2,1)S(1)}, u32[]{:S(2)}, u32[]{:S(2)}) %collective-permute-start.4) | collective-permute-done | bytes 32800 | tf_op jit(solution)/shard_map/ppermute | solution.py:426
  24.3 0.8 collective-permute-done.5.refs_9_
  25.1 15.1 %shard_map.96 = (f32[16,64,256]{2,1,0:T(8,128)}, bf16[8,16,4608]{2,1,0:T(8,128)(2,1)S(1)}, f32[8,16,4608]{2,1,0:T(8,128)S(1)}) custom-call(bf16[16,64,256]{2,1,0:T(8,128)(2,1)} %refs_0_.1, bf16[16,64,256]{2,1,0:T(8,128)(2,1)} %refs_1_.1, s32[16,64,256]{2,1,0:T(8,128)} %refs_2_.1, bf16[2304,256]{1,0:T(8,128)(2,1)} %bitcast.8, ...), custom_call_target="tpu_custom_call" | custom-call | tf_op jit(solution)/shard_map/pallas_call | solution.py:375
  40.2 4.2 %collective-permute-start.6 = (bf16[8,16,4608]{2,1,0:T(8,128)(2,1)S(1)}, bf16[8,16,4608]{2,1,0:T(8,128)(2,1)S(1)}, u32[]{:S(2)}, u32[]{:S(2)}) collective-permute-start(bf16[8,16,4608]{2,1,0:T(8,128)(2,1)S(1)} %get-tuple-element.28), channel_id=1, source_target_pairs={{0,1},{1,0},{2,3},{3,2},{4,5},{5,4},{6,7},{7,6},{8,9},{9,8},{10,11... | collective-permute-start | bytes 3538952 | tf_op jit(solution)/shard_map/ppermute | solution.py:388
  44.4 2.5 %collective-permute-done.6.got = bf16[8,16,4608]{2,1,0:T(8,128)(2,1)S(1)} collective-permute-done((bf16[8,16,4608]{2,1,0:T(8,128)(2,1)S(1)}, bf16[8,16,4608]{2,1,0:T(8,128)(2,1)S(1)}, u32[]{:S(2)}, u32[]{:S(2)}) %collective-permute-start.6) | collective-permute-done | bytes 1179680 | tf_op jit(solution)/shard_map/ppermute | solution.py:388
  46.9 0.2 shard_map.97
  47.3 1.9 %collective-permute-start.9 = (bf16[2,16,4608]{2,1,0:T(8,128)(2,1)S(1)}, bf16[2,16,4608]{2,1,0:T(8,128)(2,1)S(1)}, u32[]{:S(2)}, u32[]{:S(2)}) collective-permute-start(bf16[2,16,4608]{2,1,0:T(8,128)(2,1)S(1)} %get-tuple-element.32), channel_id=1, source_target_pairs={{0,12},{1,13},{2,14},{3,15},{4,0},{5,1},{6,2},{7,3},{8,4},{9,5},{1... | collective-permute-start | bytes 884744 | tf_op jit(solution)/shard_map/ppermute | solution.py:50
  49.2 7.8 %collective-permute-done.7.r1 = bf16[2,16,4608]{2,1,0:T(8,128)(2,1)S(1)} collective-permute-done((bf16[2,16,4608]{2,1,0:T(8,128)(2,1)S(1)}, bf16[2,16,4608]{2,1,0:T(8,128)(2,1)S(1)}, u32[]{:S(2)}, u32[]{:S(2)}) %collective-permute-start.7) | collective-permute-done | bytes 294944 | tf_op jit(solution)/shard_map/ppermute | solution.py:50
  57.0 1.6 %collective-permute-done.8.r2 = bf16[2,16,4608]{2,1,0:T(8,128)(2,1)S(1)} collective-permute-done((bf16[2,16,4608]{2,1,0:T(8,128)(2,1)S(1)}, bf16[2,16,4608]{2,1,0:T(8,128)(2,1)S(1)}, u32[]{:S(2)}, u32[]{:S(2)}) %collective-permute-start.8) | collective-permute-done | bytes 294944 | tf_op jit(solution)/shard_map/ppermute | solution.py:50
  58.7 5.7 %collective-permute-done.9.r3 = bf16[2,16,4608]{2,1,0:T(8,128)(2,1)S(1)} collective-permute-done((bf16[2,16,4608]{2,1,0:T(8,128)(2,1)S(1)}, bf16[2,16,4608]{2,1,0:T(8,128)(2,1)S(1)}, u32[]{:S(2)}, u32[]{:S(2)}) %collective-permute-start.9) | collective-permute-done | bytes 294944 | tf_op jit(solution)/shard_map/ppermute | solution.py:50
  64.4 0.3 shard_map.98
  64.8 3.5 %collective-permute-start.11 = (bf16[32,1152]{1,0:T(8,128)(2,1)S(1)}, bf16[32,1152]{1,0:T(8,128)(2,1)S(1)}, u32[]{:S(2)}, u32[]{:S(2)}) collective-permute-start(bf16[32,1152]{1,0:T(8,128)(2,1)S(1)} %get-tuple-element.35), channel_id=1, source_target_pairs={{0,2},{1,3},{2,0},{3,1},{4,6},{5,7},{6,4},{7,5},{8,10},{9,11},{10,... | collective-permute-start | bytes 221192 | tf_op jit(solution)/shard_map/ppermute | solution.py:50
  68.3 1.2 %collective-permute-start.12 = (bf16[32,1152]{1,0:T(8,128)(2,1)S(1)}, bf16[32,1152]{1,0:T(8,128)(2,1)S(1)}, u32[]{:S(2)}, u32[]{:S(2)}) collective-permute-start(bf16[32,1152]{1,0:T(8,128)(2,1)S(1)} %get-tuple-element.36), channel_id=1, source_target_pairs={{0,18},{1,19},{2,16},{3,17},{4,22},{5,23},{6,20},{7,21},{8,26},{9,... | collective-permute-start | bytes 221192 | tf_op jit(solution)/shard_map/ppermute | solution.py:50
  69.6 2.5 %collective-permute-done.11.r2 = bf16[32,1152]{1,0:T(8,128)(2,1)S(1)} collective-permute-done((bf16[32,1152]{1,0:T(8,128)(2,1)S(1)}, bf16[32,1152]{1,0:T(8,128)(2,1)S(1)}, u32[]{:S(2)}, u32[]{:S(2)}) %collective-permute-start.11) | collective-permute-done | bytes 73760 | tf_op jit(solution)/shard_map/ppermute | solution.py:50
  72.1 1.8 %collective-permute-done.12.r3 = bf16[32,1152]{1,0:T(8,128)(2,1)S(1)} collective-permute-done((bf16[32,1152]{1,0:T(8,128)(2,1)S(1)}, bf16[32,1152]{1,0:T(8,128)(2,1)S(1)}, u32[]{:S(2)}, u32[]{:S(2)}) %collective-permute-start.12) | collective-permute-done | bytes 73760 | tf_op jit(solution)/shard_map/ppermute | solution.py:50
  73.9 0.1 shard_map.99
  74.0 11.7 %all_to_all.5 = bf16[8,32,144]{2,1,0:T(8,128)(2,1)S(1)} all-to-all(bf16[8,32,144]{2,1,0:T(8,128)(2,1)S(1)} %shard_map.99), channel_id=1, replica_groups=mesh['z'=8,'yl'=2,'x'=4,'yh'=2,'core'=2] {'z'}, dimensions={0} | all-to-all | bytes 147456 | tf_op jit(solution)/shard_map/all_to_all | solution.py:402
  85.8 0.6 slice_bitcast_fusion
  (11 shorter events, 0.6 us)
Async XLA Ops:
  2.5 22.6 %collective-permute-start = (bf16[6,64,256]{2,1,0:T(8,128)(2,1)S(1)}, bf16[6,64,256]{2,1,0:T(8,128)(2,1)S(1)}, u32[]{:S(2)}, u32[]{:S(2)}) collective-permute-start(bf16[6,64,256]{2,1,0:T(8,128)(2,1)S(1)} %get-tuple-element.20), channel_id=1, source_target_pairs={{0,1},{1,2},{2,3},{3,4},{4,5},{5,6},{6,7},{7,8},{8,9},{9,10},{10,1... | collective-permute-start | bytes 589832 | tf_op jit(solution)/shard_map/ppermute | solution.py:423
  2.6 22.5 %collective-permute-start.1 = (bf16[6,64,256]{2,1,0:T(8,128)(2,1)S(1)}, bf16[6,64,256]{2,1,0:T(8,128)(2,1)S(1)}, u32[]{:S(2)}, u32[]{:S(2)}) collective-permute-start(bf16[6,64,256]{2,1,0:T(8,128)(2,1)S(1)} %get-tuple-element.21), channel_id=1, source_target_pairs={{0,128},{1,0},{2,1},{3,2},{4,3},{5,4},{6,5},{7,6},{8,7},{9,8},{10,... | collective-permute-start | bytes 589832 | tf_op jit(solution)/shard_map/ppermute | solution.py:424
  6.7 7.1 %collective-permute-start.2 = (bf16[128,256]{1,0:T(8,128)(2,1)S(1)}, bf16[128,256]{1,0:T(8,128)(2,1)S(1)}, u32[]{:S(2)}, u32[]{:S(2)}) collective-permute-start(bf16[128,256]{1,0:T(8,128)(2,1)S(1)} %get-tuple-element.22), channel_id=1, source_target_pairs={{16,0},{32,16},{48,32},{64,48},{80,64},{96,80},{112,96},{128,112},... | collective-permute-start | bytes 196616 | tf_op jit(solution)/shard_map/ppermute | solution.py:422
  11.4 7.0 %collective-permute-start.3 = (bf16[128,256]{1,0:T(8,128)(2,1)S(1)}, bf16[128,256]{1,0:T(8,128)(2,1)S(1)}, u32[]{:S(2)}, u32[]{:S(2)}) collective-permute-start(bf16[128,256]{1,0:T(8,128)(2,1)S(1)} %get-tuple-element.23), channel_id=1, source_target_pairs={{0,16},{16,32},{32,48},{48,64},{64,80},{80,96},{96,112},{112,128},... | collective-permute-start | bytes 196616 | tf_op jit(solution)/shard_map/ppermute | solution.py:421
  18.4 5.8 %collective-permute-start.4 = (bf16[64,256]{1,0:T(8,128)(2,1)S(1)}, bf16[64,256]{1,0:T(8,128)(2,1)S(1)}, u32[]{:S(2)}, u32[]{:S(2)}) collective-permute-start(bf16[64,256]{1,0:T(8,128)(2,1)S(1)} %get-tuple-element.24), channel_id=1, source_target_pairs={{0,1},{1,2},{2,3},{3,4},{4,5},{5,6},{6,7},{7,8},{8,9},{9,10},{10,1... | collective-permute-start | bytes 98312 | tf_op jit(solution)/shard_map/ppermute | solution.py:426
  18.5 6.5 %collective-permute-start.5 = (bf16[64,256]{1,0:T(8,128)(2,1)S(1)}, bf16[64,256]{1,0:T(8,128)(2,1)S(1)}, u32[]{:S(2)}, u32[]{:S(2)}) collective-permute-start(bf16[64,256]{1,0:T(8,128)(2,1)S(1)} %get-tuple-element.25), channel_id=1, source_target_pairs={{0,128},{1,0},{2,1},{3,2},{4,3},{5,4},{6,5},{7,6},{8,7},{9,8},{10,... | collective-permute-start | bytes 98312 | tf_op jit(solution)/shard_map/ppermute | solution.py:427
  40.2 6.7 %collective-permute-start.6 = (bf16[8,16,4608]{2,1,0:T(8,128)(2,1)S(1)}, bf16[8,16,4608]{2,1,0:T(8,128)(2,1)S(1)}, u32[]{:S(2)}, u32[]{:S(2)}) collective-permute-start(bf16[8,16,4608]{2,1,0:T(8,128)(2,1)S(1)} %get-tuple-element.28), channel_id=1, source_target_pairs={{0,1},{1,0},{2,3},{3,2},{4,5},{5,4},{6,7},{7,6},{8,9},{9,8},{10,11... | collective-permute-start | bytes 3538952 | tf_op jit(solution)/shard_map/ppermute | solution.py:388
  47.1 9.9 %collective-permute-start.7 = (bf16[2,16,4608]{2,1,0:T(8,128)(2,1)S(1)}, bf16[2,16,4608]{2,1,0:T(8,128)(2,1)S(1)}, u32[]{:S(2)}, u32[]{:S(2)}) collective-permute-start(bf16[2,16,4608]{2,1,0:T(8,128)(2,1)S(1)} %get-tuple-element.30), channel_id=1, source_target_pairs={{0,4},{1,5},{2,6},{3,7},{4,8},{5,9},{6,10},{7,11},{8,12},{9,13},{1... | collective-permute-start | bytes 884744 | tf_op jit(solution)/shard_map/ppermute | solution.py:50
  47.2 11.5 %collective-permute-start.8 = (bf16[2,16,4608]{2,1,0:T(8,128)(2,1)S(1)}, bf16[2,16,4608]{2,1,0:T(8,128)(2,1)S(1)}, u32[]{:S(2)}, u32[]{:S(2)}) collective-permute-start(bf16[2,16,4608]{2,1,0:T(8,128)(2,1)S(1)} %get-tuple-element.31), channel_id=1, source_target_pairs={{0,8},{1,9},{2,10},{3,11},{4,12},{5,13},{6,14},{7,15},{8,0},{9,1},... | collective-permute-start | bytes 884744 | tf_op jit(solution)/shard_map/ppermute | solution.py:50
  47.3 17.1 %collective-permute-start.9 = (bf16[2,16,4608]{2,1,0:T(8,128)(2,1)S(1)}, bf16[2,16,4608]{2,1,0:T(8,128)(2,1)S(1)}, u32[]{:S(2)}, u32[]{:S(2)}) collective-permute-start(bf16[2,16,4608]{2,1,0:T(8,128)(2,1)S(1)} %get-tuple-element.32), channel_id=1, source_target_pairs={{0,12},{1,13},{2,14},{3,15},{4,0},{5,1},{6,2},{7,3},{8,4},{9,5},{1... | collective-permute-start | bytes 884744 | tf_op jit(solution)/shard_map/ppermute | solution.py:50
  64.7 4.9 %collective-permute-start.10 = (bf16[32,1152]{1,0:T(8,128)(2,1)S(1)}, bf16[32,1152]{1,0:T(8,128)(2,1)S(1)}, u32[]{:S(2)}, u32[]{:S(2)}) collective-permute-start(bf16[32,1152]{1,0:T(8,128)(2,1)S(1)} %get-tuple-element.34), channel_id=1, source_target_pairs={{0,16},{1,17},{2,18},{3,19},{4,20},{5,21},{6,22},{7,23},{8,24},{9,... | collective-permute-start | bytes 221192 | tf_op jit(solution)/shard_map/ppermute | solution.py:50
  64.8 7.3 %collective-permute-start.11 = (bf16[32,1152]{1,0:T(8,128)(2,1)S(1)}, bf16[32,1152]{1,0:T(8,128)(2,1)S(1)}, u32[]{:S(2)}, u32[]{:S(2)}) collective-permute-start(bf16[32,1152]{1,0:T(8,128)(2,1)S(1)} %get-tuple-element.35), channel_id=1, source_target_pairs={{0,2},{1,3},{2,0},{3,1},{4,6},{5,7},{6,4},{7,5},{8,10},{9,11},{10,... | collective-permute-start | bytes 221192 | tf_op jit(solution)/shard_map/ppermute | solution.py:50
  68.3 5.6 %collective-permute-start.12 = (bf16[32,1152]{1,0:T(8,128)(2,1)S(1)}, bf16[32,1152]{1,0:T(8,128)(2,1)S(1)}, u32[]{:S(2)}, u32[]{:S(2)}) collective-permute-start(bf16[32,1152]{1,0:T(8,128)(2,1)S(1)} %get-tuple-element.36), channel_id=1, source_target_pairs={{0,18},{1,19},{2,16},{3,17},{4,22},{5,23},{6,20},{7,21},{8,26},{9,... | collective-permute-start | bytes 221192 | tf_op jit(solution)/shard_map/ppermute | solution.py:50

commit v4 on v3

--- a/solution.py
+++ b/solution.py
@@ -85,8 +85,8 @@
     cotangent = cotangent_of(levels, prior)
 
     def outward(k, first, last):
-        cw[k] = jnp.where(low, last, first).astype(BF16)
-        ccw[k] = jnp.where(low, first, last).astype(BF16)
+        cw[COLS * k : COLS * (k + 1), :] = jnp.where(low, last, first).astype(BF16)
+        ccw[COLS * k : COLS * (k + 1), :] = jnp.where(low, first, last).astype(BF16)
 
     for k in range(4):
         outward(k, latent[k].astype(F32), latent[12 + k].astype(F32))
@@ -114,20 +114,24 @@
         out[...] = jnp.where(spot < 4, x, q).astype(BF16)
 
 
-def corners_kernel(from_west, from_east, cw_corner, ccw_corner):
+def corners_kernel(from_west, from_east, cw_rows, ccw_rows, cw, ccw):
     lon, lat = place()
     low = lon < 8
+    cw[0:384, :] = cw_rows[...]
+    ccw[0:384, :] = ccw_rows[...]
     for side, strip in enumerate((from_west, from_east)):
+        at = 384 + 32 * side
         first, last = strip[0:32, :].astype(F32), strip[96:128, :].astype(F32)
-        cw_corner[32 * side : 32 * side + 32, :] = jnp.where(low, last, first).astype(BF16)
-        ccw_corner[32 * side : 32 * side + 32, :] = jnp.where(low, first, last).astype(BF16)
+        cw[at : at + 32, :] = jnp.where(low, last, first).astype(BF16)
+        ccw[at : at + 32, :] = jnp.where(low, first, last).astype(BF16)
 
 
 def facing(first, second, low, rows, count, mirrored):
     picked = []
     for k in range(count):
-        at = rows + jnp.where(mirrored, count - 1 - k, k)
-        picked.append(jnp.where(low, first[at].astype(F32), second[at].astype(F32)))
+        at = pl.multiple_of((rows + jnp.where(mirrored, count - 1 - k, k)) * COLS, COLS)
+        one, two = first[pl.ds(at, COLS), :], second[pl.ds(at, COLS), :]
+        picked.append(jnp.where(low, one.astype(F32), two.astype(F32)))
     return picked
 
 
@@ -151,14 +155,14 @@
 
 
 def block_kernel(*refs):
-    fars = refs[:13]
-    grad_latent, send, keep = refs[13:16]
-    nears = refs[16:29]
-    x32, q32, a32, g32, dact, lat3, act3, go3, gp3, turn, arrived = refs[29:]
+    fars = refs[:11]
+    grad_latent, send, keep = refs[11:14]
+    nears = refs[14:25]
+    x32, q32, a32, g32, dact, lat3, act3, go3, gp3, turn, arrived = refs[25:]
     fetches = fetched(tuple(zip(fars, nears)), arrived)
-    latent, code, bins, w1, cw, ccw, from_east, from_west, cw_corner, ccw_corner, levels, prior, w2 = nears
+    latent, code, bins, w1, cw, ccw, from_east, from_west, levels, prior, w2 = nears
     p32 = a32
-    for fetch in fetches[:3] + fetches[4:12]:
+    for fetch in fetches[:3] + fetches[4:10]:
         fetch.wait()
     lon, lat = place()
     low = lon < 8
@@ -186,8 +190,8 @@
     spot = lax.broadcasted_iota(jnp.int32, (rows, C), 0) % 8
 
     def column(own, side):
-        one = cw_corner[32 * side : 32 * side + 32, :].astype(F32)
-        two = ccw_corner[32 * side : 32 * side + 32, :].astype(F32)
+        at = 384 + 32 * side
+        one, two = cw[at : at + 32, :].astype(F32), ccw[at : at + 32, :].astype(F32)
 
         def end(value, mirrored):
             tiles = [value[8 * k : 8 * k + 8] for k in range(4)]
@@ -276,7 +280,7 @@
         put(a32, at + skip, pre * sig)
 
     spread(act3, a32, W, 23 * W + 16)
-    fetches[12].wait()
+    fetches[10].wait()
     for at, count, skip, order in pieces(2, 22, 4, 20, (top_flip, low_flip)):
         conv = product(act3, at, count, w2, order)[skip:]
         size = count - skip
@@ -408,9 +412,9 @@
     levels = levels.reshape(1, C)
     prior = prior_scale.reshape(1, C)
     given = [pltpu.with_memory_space_constraint(v, pltpu.HBM) for v in (latent, code_grad, bins, levels, prior)]
-    edge = ((6, COLS, C), BF16)
+    edge = ((6 * COLS, C), BF16)
     strip = ((ROWS * 8, C), BF16)
-    corner = ((64, C), BF16)
+    message = ((6 * COLS + 64, C), BF16)
     cells = (ROWS, COLS, C)
     cw, ccw, east, west = local_call(
         rims_kernel,
@@ -420,22 +424,20 @@
     )(*given)
     from_west = lax.ppermute(east, ("z", "yl"), [(i, (i + 1) % 16) for i in range(16)])
     from_east = lax.ppermute(west, ("z", "yl"), [((i + 1) % 16, i) for i in range(16)])
+    cw, ccw = local_call(corners_kernel, [message] * 2)(from_west, from_east, cw, ccw)
     cw = lax.ppermute(cw, FINE, ring_pairs(1))
     ccw = lax.ppermute(ccw, FINE, ring_pairs(-1))
-    cw_corner, ccw_corner = local_call(corners_kernel, [corner] * 2)(from_west, from_east)
-    cw_corner = lax.ppermute(cw_corner, FINE, ring_pairs(1))
-    ccw_corner = lax.ppermute(ccw_corner, FINE, ring_pairs(-1))
 
     frame = pltpu.VMEM((2, N + 2 * BASE, 128), F32)
     triple = pltpu.VMEM((N, 3 * C), BF16)
     w1, w2 = [pltpu.with_memory_space_constraint(w.reshape(TAPS, C), pltpu.HBM) for w in (w_first, w_second)]
-    fars = given[:3] + [w1, cw, ccw, from_east, from_west, cw_corner, ccw_corner] + given[3:] + [w2]
+    fars = given[:3] + [w1, cw, ccw, from_east, from_west] + given[3:] + [w2]
     grad_latent, send, keep = local_call(
         block_kernel,
         [(cells, F32), ((8, 16, 2 * TAPS), BF16), ((8, 16, 2 * TAPS), F32)],
         [pltpu.VMEM(v.shape, v.dtype) for v in fars]
-        + [frame] * 5 + [triple] * 4 + [pltpu.VMEM((C, ROWS * COLS), BF16), pltpu.SemaphoreType.DMA((13,))],
-        near=False, room=44, far_ins=range(13), near_outs=(1, 2),
+        + [frame] * 5 + [triple] * 4 + [pltpu.VMEM((C, ROWS * COLS), BF16), pltpu.SemaphoreType.DMA((11,))],
+        near=False, room=44, far_ins=range(11), near_outs=(1, 2),
     )(*fars)
     grad_first, grad_second = summed(send, keep)
     return (grad_latent, grad_first, grad_second)

time: 86.5 us -> 83.9 us (0.970)
  waiting for transfers between devices: 31.4 us -> 28.1 us
  blocking collectives: 11.7 us -> 12.7 us
    ppermute x2 -> x0, starting transfers between devices: 4.22 us -> none  [the longest x1 4.14 us: on_device(): ccw_corner = lax.ppermute(ccw_corner, FINE, ring_pairs(-1))]
    ppermute x1, waiting for transfers between devices: 0.01 us -> 3.72 us  [on_device(): cw = lax.ppermute(cw, FINE, ring_pairs(1))]
    ppermute x6, starting transfers between devices: 6.88 us -> 10.4 us  [moved(): return lax.ppermute(block, FINE, pairs)]
    ppermute x1, waiting for transfers between devices: 4.61 us -> 2.16 us  [on_device(): lax.ppermute(east, ('z', 'yl'), [(i, (i + 1) % 16) for i in range(16)])]
    ppermute x2 -> x0, waiting for transfers between devices: 2.39 us -> none  [the longest x1 1.59 us: on_device(): cw_corner = lax.ppermute(cw_corner, FINE, ring_pairs(1))]
    ppermute x1, waiting for transfers between devices: 2.37 us -> 0.01 us  [on_device(): lax.ppermute(west, ('z', 'yl'), [((i + 1) % 16, i) for i in range(16)])]
    ppermute x1, starting transfers between devices: 4.23 us -> 2.34 us  [summed(): got = lax.ppermute(send, 'core', [(0, 1), (1, 0)])]
    ppermute x1, starting transfers between devices: 0.01 us -> 1.65 us  [on_device(): lax.ppermute(east, ('z', 'yl'), [(i, (i + 1) % 16) for i in range(16)])]
  transfers between devices with their start and end apart: 13 -> 11, of which waited for: 11 -> 8; matrix products, arithmetic and copies ran while one was open for 0% -> 0% of each run, Pallas kernels for 0% -> 0%
where the time goes in v4:
time: 83.9 us; the launch traced here: 83.8 us
  waiting for transfers between devices  28.1 us (33%)
  starting transfers between devices  24 us (29%)
  Pallas kernels  17.6 us (21%)
  blocking collectives  12.7 us (15%)
    ppermute x6, waiting for transfers between devices, moved(): return lax.ppermute(block, FINE, pairs)  19.8 us
    pallas_call x6, Pallas kernels, call(): pl.pallas_call(kernel, out_shape=shapes, in_specs=[far if i in far_ins el...  17.6 us
    all_to_all x1, blocking collectives, summed(): parts = lax.all_to_all(parts, 'z', 0, 0)  12.7 us
    ppermute x6, starting transfers between devices, moved(): return lax.ppermute(block, FINE, pairs)  10.4 us
    ppermute x1, starting transfers between devices, on_device(): lax.ppermute(west, ('z', 'yl'), [((i + 1) % 16, i) for i in range(16)])  5.38 us
    ppermute x1, starting transfers between devices, on_device(): ccw = lax.ppermute(ccw, FINE, ring_pairs(-1))  4.14 us
    ppermute x1, waiting for transfers between devices, on_device(): cw = lax.ppermute(cw, FINE, ring_pairs(1))  3.72 us
    ppermute x1, waiting for transfers between devices, summed(): got = lax.ppermute(send, 'core', [(0, 1), (1, 0)])  2.47 us
  transfers between devices with their start and end apart: 11, of which 8 were waited for; matrix products, arithmetic and copies ran while one was open for 0% of the time, Pallas kernels for 0%

profile of v4, /device:TPU:6, one launch (start us, length us, event | category | flops | bytes accessed | tf_op | source)
XLA Modules:
  0.0 83.8 jit_solution(10534972865035383796)
XLA Ops:
  0.6 1.9 %shard_map.94 = (bf16[384,256]{1,0:T(8,128)(2,1)S(1)}, bf16[384,256]{1,0:T(8,128)(2,1)S(1)}, bf16[128,256]{1,0:T(8,128)(2,1)S(1)}, bf16[128,256]{1,0:T(8,128)(2,1)S(1)}) custom-call(bf16[16,64,256]{2,1,0:T(8,128)(2,1)} %refs_0_.1, bf16[16,64,256]{2,1,0:T(8,128)(2,1)} %refs_1_.1, s32[16,64,256]{2,1,0:T(8,128)} %refs_2_.1, s32[1,256]{1,0:T(1,128)} %bitcast.10, ...), custom_call_target="tpu_custom_call" | custom-call | tf_op jit(solution)/shard_map/pallas_call | solution.py:379
  2.5 1.7 %collective-permute-start = (bf16[128,256]{1,0:T(8,128)(2,1)S(1)}, bf16[128,256]{1,0:T(8,128)(2,1)S(1)}, u32[]{:S(2)}, u32[]{:S(2)}) collective-permute-start(bf16[128,256]{1,0:T(8,128)(2,1)S(1)} %get-tuple-element.20), channel_id=1, source_target_pairs={{0,16},{16,32},{32,48},{48,64},{64,80},{80,96},{96,112},{112,128},... | collective-permute-start | bytes 196616 | tf_op jit(solution)/shard_map/ppermute | solution.py:425
  4.1 5.4 %collective-permute-start.1 = (bf16[128,256]{1,0:T(8,128)(2,1)S(1)}, bf16[128,256]{1,0:T(8,128)(2,1)S(1)}, u32[]{:S(2)}, u32[]{:S(2)}) collective-permute-start(bf16[128,256]{1,0:T(8,128)(2,1)S(1)} %get-tuple-element.21), channel_id=1, source_target_pairs={{16,0},{32,16},{48,32},{64,48},{80,64},{96,80},{112,96},{128,112},... | collective-permute-start | bytes 196616 | tf_op jit(solution)/shard_map/ppermute | solution.py:426
  9.5 2.2 %collective-permute-done.from_west.refs_7_ = bf16[128,256]{1,0:T(8,128)(2,1)S(1)} collective-permute-done((bf16[128,256]{1,0:T(8,128)(2,1)S(1)}, bf16[128,256]{1,0:T(8,128)(2,1)S(1)}, u32[]{:S(2)}, u32[]{:S(2)}) %collective-permute-start) | collective-permute-done | bytes 65568 | tf_op jit(solution)/shard_map/ppermute | solution.py:425
  11.8 4.1 %collective-permute-start.3 = (bf16[448,256]{1,0:T(8,128)(2,1)S(1)}, bf16[448,256]{1,0:T(8,128)(2,1)S(1)}, u32[]{:S(2)}, u32[]{:S(2)}) collective-permute-start(bf16[448,256]{1,0:T(8,128)(2,1)S(1)} %get-tuple-element.25), channel_id=1, source_target_pairs={{0,128},{1,0},{2,1},{3,2},{4,3},{5,4},{6,5},{7,6},{8,7},{9,8},{10,... | collective-permute-start | bytes 688136 | tf_op jit(solution)/shard_map/ppermute | solution.py:429
  16.0 3.7 %collective-permute-done.2.refs_4_ = bf16[448,256]{1,0:T(8,128)(2,1)S(1)} collective-permute-done((bf16[448,256]{1,0:T(8,128)(2,1)S(1)}, bf16[448,256]{1,0:T(8,128)(2,1)S(1)}, u32[]{:S(2)}, u32[]{:S(2)}) %collective-permute-start.2) | collective-permute-done | bytes 229408 | tf_op jit(solution)/shard_map/ppermute | solution.py:428
  19.7 15.1 %shard_map.96 = (f32[16,64,256]{2,1,0:T(8,128)}, bf16[8,16,4608]{2,1,0:T(8,128)(2,1)S(1)}, f32[8,16,4608]{2,1,0:T(8,128)S(1)}) custom-call(bf16[16,64,256]{2,1,0:T(8,128)(2,1)} %refs_0_.1, bf16[16,64,256]{2,1,0:T(8,128)(2,1)} %refs_1_.1, s32[16,64,256]{2,1,0:T(8,128)} %refs_2_.1, bf16[2304,256]{1,0:T(8,128)(2,1)} %bitcast.8, ...), custom_call_target="tpu_custom_call" | custom-call | tf_op jit(solution)/shard_map/pallas_call | solution.py:379
  34.8 2.3 %collective-permute-start.4 = (bf16[8,16,4608]{2,1,0:T(8,128)(2,1)S(1)}, bf16[8,16,4608]{2,1,0:T(8,128)(2,1)S(1)}, u32[]{:S(2)}, u32[]{:S(2)}) collective-permute-start(bf16[8,16,4608]{2,1,0:T(8,128)(2,1)S(1)} %get-tuple-element.28), channel_id=1, source_target_pairs={{0,1},{1,0},{2,3},{3,2},{4,5},{5,4},{6,7},{7,6},{8,9},{9,8},{10,11... | collective-permute-start | bytes 3538952 | tf_op jit(solution)/shard_map/ppermute | solution.py:392
  37.1 2.5 %collective-permute-done.4.got = bf16[8,16,4608]{2,1,0:T(8,128)(2,1)S(1)} collective-permute-done((bf16[8,16,4608]{2,1,0:T(8,128)(2,1)S(1)}, bf16[8,16,4608]{2,1,0:T(8,128)(2,1)S(1)}, u32[]{:S(2)}, u32[]{:S(2)}) %collective-permute-start.4) | collective-permute-done | bytes 1179680 | tf_op jit(solution)/shard_map/ppermute | solution.py:392
  39.6 0.2 shard_map.97
  39.8 0.8 %collective-permute-start.5 = (bf16[2,16,4608]{2,1,0:T(8,128)(2,1)S(1)}, bf16[2,16,4608]{2,1,0:T(8,128)(2,1)S(1)}, u32[]{:S(2)}, u32[]{:S(2)}) collective-permute-start(bf16[2,16,4608]{2,1,0:T(8,128)(2,1)S(1)} %get-tuple-element.30), channel_id=1, source_target_pairs={{0,4},{1,5},{2,6},{3,7},{4,8},{5,9},{6,10},{7,11},{8,12},{9,13},{1... | collective-permute-start | bytes 884744 | tf_op jit(solution)/shard_map/ppermute | solution.py:50
  40.6 2.2 %collective-permute-start.6 = (bf16[2,16,4608]{2,1,0:T(8,128)(2,1)S(1)}, bf16[2,16,4608]{2,1,0:T(8,128)(2,1)S(1)}, u32[]{:S(2)}, u32[]{:S(2)}) collective-permute-start(bf16[2,16,4608]{2,1,0:T(8,128)(2,1)S(1)} %get-tuple-element.31), channel_id=1, source_target_pairs={{0,8},{1,9},{2,10},{3,11},{4,12},{5,13},{6,14},{7,15},{8,0},{9,1},... | collective-permute-start | bytes 884744 | tf_op jit(solution)/shard_map/ppermute | solution.py:50
  42.8 6.9 %collective-permute-done.5.r1 = bf16[2,16,4608]{2,1,0:T(8,128)(2,1)S(1)} collective-permute-done((bf16[2,16,4608]{2,1,0:T(8,128)(2,1)S(1)}, bf16[2,16,4608]{2,1,0:T(8,128)(2,1)S(1)}, u32[]{:S(2)}, u32[]{:S(2)}) %collective-permute-start.5) | collective-permute-done | bytes 294944 | tf_op jit(solution)/shard_map/ppermute | solution.py:50
  49.7 2.4 %collective-permute-done.6.r2 = bf16[2,16,4608]{2,1,0:T(8,128)(2,1)S(1)} collective-permute-done((bf16[2,16,4608]{2,1,0:T(8,128)(2,1)S(1)}, bf16[2,16,4608]{2,1,0:T(8,128)(2,1)S(1)}, u32[]{:S(2)}, u32[]{:S(2)}) %collective-permute-start.6) | collective-permute-done | bytes 294944 | tf_op jit(solution)/shard_map/ppermute | solution.py:50
  52.1 5.2 %collective-permute-done.7.r3 = bf16[2,16,4608]{2,1,0:T(8,128)(2,1)S(1)} collective-permute-done((bf16[2,16,4608]{2,1,0:T(8,128)(2,1)S(1)}, bf16[2,16,4608]{2,1,0:T(8,128)(2,1)S(1)}, u32[]{:S(2)}, u32[]{:S(2)}) %collective-permute-start.7) | collective-permute-done | bytes 294944 | tf_op jit(solution)/shard_map/ppermute | solution.py:50
  57.2 0.3 shard_map.98
  57.6 1.7 %collective-permute-start.8 = (bf16[32,1152]{1,0:T(8,128)(2,1)S(1)}, bf16[32,1152]{1,0:T(8,128)(2,1)S(1)}, u32[]{:S(2)}, u32[]{:S(2)}) collective-permute-start(bf16[32,1152]{1,0:T(8,128)(2,1)S(1)} %get-tuple-element.34), channel_id=1, source_target_pairs={{0,16},{1,17},{2,18},{3,19},{4,20},{5,21},{6,22},{7,23},{8,24},{9,... | collective-permute-start | bytes 221192 | tf_op jit(solution)/shard_map/ppermute | solution.py:50
  59.3 5.5 %collective-permute-start.9 = (bf16[32,1152]{1,0:T(8,128)(2,1)S(1)}, bf16[32,1152]{1,0:T(8,128)(2,1)S(1)}, u32[]{:S(2)}, u32[]{:S(2)}) collective-permute-start(bf16[32,1152]{1,0:T(8,128)(2,1)S(1)} %get-tuple-element.35), channel_id=1, source_target_pairs={{0,2},{1,3},{2,0},{3,1},{4,6},{5,7},{6,4},{7,5},{8,10},{9,11},{10,... | collective-permute-start | bytes 221192 | tf_op jit(solution)/shard_map/ppermute | solution.py:50
  64.8 0.2 collective-permute-start.10
  65.0 3.6 %collective-permute-done.9.r2 = bf16[32,1152]{1,0:T(8,128)(2,1)S(1)} collective-permute-done((bf16[32,1152]{1,0:T(8,128)(2,1)S(1)}, bf16[32,1152]{1,0:T(8,128)(2,1)S(1)}, u32[]{:S(2)}, u32[]{:S(2)}) %collective-permute-start.9) | collective-permute-done | bytes 73760 | tf_op jit(solution)/shard_map/ppermute | solution.py:50
  68.6 1.8 %collective-permute-done.10.r3 = bf16[32,1152]{1,0:T(8,128)(2,1)S(1)} collective-permute-done((bf16[32,1152]{1,0:T(8,128)(2,1)S(1)}, bf16[32,1152]{1,0:T(8,128)(2,1)S(1)}, u32[]{:S(2)}, u32[]{:S(2)}) %collective-permute-start.10) | collective-permute-done | bytes 73760 | tf_op jit(solution)/shard_map/ppermute | solution.py:50
  70.4 0.1 shard_map.99
  70.5 12.7 %all_to_all.5 = bf16[8,32,144]{2,1,0:T(8,128)(2,1)S(1)} all-to-all(bf16[8,32,144]{2,1,0:T(8,128)(2,1)S(1)} %shard_map.99), channel_id=1, replica_groups=mesh['z'=8,'yl'=2,'x'=4,'yh'=2,'core'=2] {'z'}, dimensions={0} | all-to-all | bytes 147456 | tf_op jit(solution)/shard_map/all_to_all | solution.py:406
  83.2 0.6 slice_bitcast_fusion
  (7 shorter events, 0.2 us)
Async XLA Ops:
  2.5 9.2 %collective-permute-start = (bf16[128,256]{1,0:T(8,128)(2,1)S(1)}, bf16[128,256]{1,0:T(8,128)(2,1)S(1)}, u32[]{:S(2)}, u32[]{:S(2)}) collective-permute-start(bf16[128,256]{1,0:T(8,128)(2,1)S(1)} %get-tuple-element.20), channel_id=1, source_target_pairs={{0,16},{16,32},{32,48},{48,64},{64,80},{80,96},{96,112},{112,128},... | collective-permute-start | bytes 196616 | tf_op jit(solution)/shard_map/ppermute | solution.py:425
  4.1 7.5 %collective-permute-start.1 = (bf16[128,256]{1,0:T(8,128)(2,1)S(1)}, bf16[128,256]{1,0:T(8,128)(2,1)S(1)}, u32[]{:S(2)}, u32[]{:S(2)}) collective-permute-start(bf16[128,256]{1,0:T(8,128)(2,1)S(1)} %get-tuple-element.21), channel_id=1, source_target_pairs={{16,0},{32,16},{48,32},{64,48},{80,64},{96,80},{112,96},{128,112},... | collective-permute-start | bytes 196616 | tf_op jit(solution)/shard_map/ppermute | solution.py:426
  11.7 7.9 %collective-permute-start.2 = (bf16[448,256]{1,0:T(8,128)(2,1)S(1)}, bf16[448,256]{1,0:T(8,128)(2,1)S(1)}, u32[]{:S(2)}, u32[]{:S(2)}) collective-permute-start(bf16[448,256]{1,0:T(8,128)(2,1)S(1)} %get-tuple-element.24), channel_id=1, source_target_pairs={{0,1},{1,2},{2,3},{3,4},{4,5},{5,6},{6,7},{7,8},{8,9},{9,10},{10,1... | collective-permute-start | bytes 688136 | tf_op jit(solution)/shard_map/ppermute | solution.py:428
  11.8 7.9 %collective-permute-start.3 = (bf16[448,256]{1,0:T(8,128)(2,1)S(1)}, bf16[448,256]{1,0:T(8,128)(2,1)S(1)}, u32[]{:S(2)}, u32[]{:S(2)}) collective-permute-start(bf16[448,256]{1,0:T(8,128)(2,1)S(1)} %get-tuple-element.25), channel_id=1, source_target_pairs={{0,128},{1,0},{2,1},{3,2},{4,3},{5,4},{6,5},{7,6},{8,7},{9,8},{10,... | collective-permute-start | bytes 688136 | tf_op jit(solution)/shard_map/ppermute | solution.py:429
  34.8 4.8 %collective-permute-start.4 = (bf16[8,16,4608]{2,1,0:T(8,128)(2,1)S(1)}, bf16[8,16,4608]{2,1,0:T(8,128)(2,1)S(1)}, u32[]{:S(2)}, u32[]{:S(2)}) collective-permute-start(bf16[8,16,4608]{2,1,0:T(8,128)(2,1)S(1)} %get-tuple-element.28), channel_id=1, source_target_pairs={{0,1},{1,0},{2,3},{3,2},{4,5},{5,4},{6,7},{7,6},{8,9},{9,8},{10,11... | collective-permute-start | bytes 3538952 | tf_op jit(solution)/shard_map/ppermute | solution.py:392
  39.8 9.9 %collective-permute-start.5 = (bf16[2,16,4608]{2,1,0:T(8,128)(2,1)S(1)}, bf16[2,16,4608]{2,1,0:T(8,128)(2,1)S(1)}, u32[]{:S(2)}, u32[]{:S(2)}) collective-permute-start(bf16[2,16,4608]{2,1,0:T(8,128)(2,1)S(1)} %get-tuple-element.30), channel_id=1, source_target_pairs={{0,4},{1,5},{2,6},{3,7},{4,8},{5,9},{6,10},{7,11},{8,12},{9,13},{1... | collective-permute-start | bytes 884744 | tf_op jit(solution)/shard_map/ppermute | solution.py:50
  40.6 11.4 %collective-permute-start.6 = (bf16[2,16,4608]{2,1,0:T(8,128)(2,1)S(1)}, bf16[2,16,4608]{2,1,0:T(8,128)(2,1)S(1)}, u32[]{:S(2)}, u32[]{:S(2)}) collective-permute-start(bf16[2,16,4608]{2,1,0:T(8,128)(2,1)S(1)} %get-tuple-element.31), channel_id=1, source_target_pairs={{0,8},{1,9},{2,10},{3,11},{4,12},{5,13},{6,14},{7,15},{8,0},{9,1},... | collective-permute-start | bytes 884744 | tf_op jit(solution)/shard_map/ppermute | solution.py:50
  42.8 14.4 %collective-permute-start.7 = (bf16[2,16,4608]{2,1,0:T(8,128)(2,1)S(1)}, bf16[2,16,4608]{2,1,0:T(8,128)(2,1)S(1)}, u32[]{:S(2)}, u32[]{:S(2)}) collective-permute-start(bf16[2,16,4608]{2,1,0:T(8,128)(2,1)S(1)} %get-tuple-element.32), channel_id=1, source_target_pairs={{0,12},{1,13},{2,14},{3,15},{4,0},{5,1},{6,2},{7,3},{8,4},{9,5},{1... | collective-permute-start | bytes 884744 | tf_op jit(solution)/shard_map/ppermute | solution.py:50
  57.6 7.4 %collective-permute-start.8 = (bf16[32,1152]{1,0:T(8,128)(2,1)S(1)}, bf16[32,1152]{1,0:T(8,128)(2,1)S(1)}, u32[]{:S(2)}, u32[]{:S(2)}) collective-permute-start(bf16[32,1152]{1,0:T(8,128)(2,1)S(1)} %get-tuple-element.34), channel_id=1, source_target_pairs={{0,16},{1,17},{2,18},{3,19},{4,20},{5,21},{6,22},{7,23},{8,24},{9,... | collective-permute-start | bytes 221192 | tf_op jit(solution)/shard_map/ppermute | solution.py:50
  59.3 9.3 %collective-permute-start.9 = (bf16[32,1152]{1,0:T(8,128)(2,1)S(1)}, bf16[32,1152]{1,0:T(8,128)(2,1)S(1)}, u32[]{:S(2)}, u32[]{:S(2)}) collective-permute-start(bf16[32,1152]{1,0:T(8,128)(2,1)S(1)} %get-tuple-element.35), channel_id=1, source_target_pairs={{0,2},{1,3},{2,0},{3,1},{4,6},{5,7},{6,4},{7,5},{8,10},{9,11},{10,... | collective-permute-start | bytes 221192 | tf_op jit(solution)/shard_map/ppermute | solution.py:50
  64.8 5.6 %collective-permute-start.10 = (bf16[32,1152]{1,0:T(8,128)(2,1)S(1)}, bf16[32,1152]{1,0:T(8,128)(2,1)S(1)}, u32[]{:S(2)}, u32[]{:S(2)}) collective-permute-start(bf16[32,1152]{1,0:T(8,128)(2,1)S(1)} %get-tuple-element.36), channel_id=1, source_target_pairs={{0,18},{1,19},{2,16},{3,17},{4,22},{5,23},{6,20},{7,21},{8,26},{9,... | collective-permute-start | bytes 221192 | tf_op jit(solution)/shard_map/ppermute | solution.py:50
